TPU v7x, 256 devices: a whole 4x4x8 slice. The times are simulated.
256 devices in a mesh: rep: 8 (over x, core), fsdp: 32 (over y, z).
Axes of the slice: x: 4, y: 4, z: 8, core: 2. Of those that a mesh axis runs over, the one named last changes fastest.
Arguments:
- tokens: bfloat16 [65536, 4608], P(('rep', 'fsdp')), may hold values from -24 to 24
- cotangent: bfloat16 [65536, 1024], P(('rep', 'fsdp')), may hold values from -0.0625 to 0.0625
- weight: bfloat16 [4608, 1024], P('fsdp'), may hold values from -0.09375 to 0.09375
- momentum: float32 [8, 4608, 1024], P('rep', 'fsdp'), may hold values from -6 to 6
- lengths: int32 [256], P(('rep', 'fsdp')), may hold values from 1 to 256, as said below
- kept_index: int32 [4608, 256], P('fsdp'), may hold values from 0 to 31, as said below
Outputs:
- projected: bfloat16 [65536, 1024], P(('rep', 'fsdp'))
- new_momentum: float32 [8, 4608, 1024], P('rep', 'fsdp')
- update: float32 [4608, 1024], P('fsdp')
Inputs may be any that keep to these rules, and one draw needn't show every extreme that they name: `lengths`: some sample has exactly 256 live tokens. `kept_index`: the 16 indices of one piece are distinct.
All inputs are finite; a program needn't handle non-finite values.
Results may differ from a plain program's by a relative error of at most 0.014.
Values may be sent and summed in bfloat16 or wider, within the bound.
No kernel may reach another device: no remote copies, remote signals or barrier semaphores. Data moves between devices by JAX's collectives and lax.ppermute only.
A program may use at most 128 MiB of HBM per device.

v0:
```python
import functools

import jax
import jax.numpy as jnp
import numpy as np
from jax import lax
from jax.experimental import pallas as pl
from jax.experimental.pallas import tpu as pltpu
from jax.sharding import Mesh, PartitionSpec as P

PIECE = 64
TOPK = 16
FREQ = 32
SLOT = 256
GROUP = 128 // FREQ * PIECE

HALVES = 2

BF16 = jnp.bfloat16
F32 = jnp.float32
HIGHEST = lax.Precision.HIGHEST
VMEM = pl.BlockSpec(memory_space=pltpu.VMEM)
SMEM = pl.BlockSpec(memory_space=pltpu.SMEM)
HBM = pl.BlockSpec(memory_space=pltpu.HBM)
PARAMS = pltpu.CompilerParams(vmem_limit_bytes=14 * 1024 * 1024)
ALL = pltpu.CompilerParams(vmem_limit_bytes=56 * 1024 * 1024)
BIG = pltpu.CompilerParams(vmem_limit_bytes=28 * 1024 * 1024)


def group_table():
    k = np.arange(FREQ)[:, None].astype(np.float64)
    n = np.arange(PIECE)[None, :].astype(np.float64)
    scale = np.where(k == 0, np.sqrt(1.0 / PIECE), np.sqrt(2.0 / PIECE))
    rows = scale * np.cos(np.pi * (2 * n + 1) * k / (2 * PIECE))
    return jnp.asarray(np.kron(np.eye(GROUP // PIECE), rows.T), F32)


def mask_rows(cot, length):
    position = lax.broadcasted_iota(jnp.int32, cot.shape, 0)
    return jnp.where(position < length, cot, jnp.zeros_like(cot))


def split_kernel(order, y_ref, length_ref, tok_ref, cot_ref, *refs):
    count = len(order)
    outs, bufs, (cot_buffer, in_sems, out_sems) = refs[:count], refs[count : 2 * count], refs[2 * count :]
    width = outs[0].shape[1] - cot_ref.shape[1]
    cot_copy = pltpu.make_async_copy(cot_ref, cot_buffer, in_sems.at[count])
    cot_copy.start()
    in_copies, out_copies = [], []
    for i, d in enumerate(order):
        start = pl.multiple_of(lax.bitwise_xor(y_ref[0], d) * width, width)
        copy = pltpu.make_async_copy(tok_ref.at[:, pl.ds(start, width)], bufs[i].at[:, :width], in_sems.at[i])
        copy.start()
        in_copies.append(copy)
        out_copies.append(pltpu.make_async_copy(bufs[i], outs[i], out_sems.at[i]))
    cot_copy.wait()
    masked = mask_rows(cot_buffer[...], length_ref[0])
    for buf, in_copy, out_copy in zip(bufs, in_copies, out_copies):
        buf[:, width:] = masked
        in_copy.wait()
        out_copy.start()
    for copy in out_copies:
        copy.wait()


def split_inputs(y, lengths, tokens, cotangent, ny, order):
    rows, width = tokens.shape[0], tokens.shape[1] // ny
    shape = (rows, width + cotangent.shape[1])
    count = len(order)
    return pl.pallas_call(
        functools.partial(split_kernel, order),
        out_shape=[jax.ShapeDtypeStruct(shape, BF16)] * count,
        in_specs=[SMEM, SMEM] + [HBM] * 2,
        out_specs=[pl.BlockSpec(memory_space=pl.ANY)] * count,
        scratch_shapes=[pltpu.VMEM(shape, BF16)] * count
        + [
            pltpu.VMEM(cotangent.shape, BF16),
            pltpu.SemaphoreType.DMA((count + 1,)),
            pltpu.SemaphoreType.DMA((count,)),
        ],
        compiler_params=ALL,
    )(y, lengths, tokens, cotangent)


def whole(array):
    return pl.BlockSpec(array.shape, lambda i, *scalars: (0,) * array.ndim)


def own_columns(tokens, ny):
    return pl.BlockSpec((tokens.shape[0], tokens.shape[1] // ny), lambda i, y, *scalars: (0, y[0]))


def contract_rows(left, right):
    return lax.dot_general(left, right, (((0,), (0,)), ((), ())), preferred_element_type=F32)


def grad_first_kernel(y_ref, length_ref, own_ref, cot_ref, both_ref, after_ref, acc_ref):
    width = own_ref.shape[1]
    acc_ref[...] = contract_rows(own_ref[...], mask_rows(cot_ref[...], length_ref[0]))
    acc_ref[...] = acc_ref[...] + contract_rows(both_ref[:, :width], both_ref[:, width:])


def grad_first(y, lengths, tokens, cotangent, both, ny, after):
    shape = (tokens.shape[1] // ny, cotangent.shape[1])
    return pl.pallas_call(
        grad_first_kernel,
        out_shape=jax.ShapeDtypeStruct(shape, F32),
        grid_spec=pltpu.PrefetchScalarGridSpec(
            num_scalar_prefetch=2,
            grid=(1,),
            in_specs=[
                own_columns(tokens, ny),
                whole(cotangent),
                whole(both),
                pl.BlockSpec(memory_space=pl.ANY),
            ],
            out_specs=pl.BlockSpec(shape, lambda i, *scalars: (0, 0)),
        ),
        compiler_params=BIG,
    )(y, lengths, tokens, cotangent, both, after)


def grad_kernel(nz, skip, place_ref, first_ref, one_ref, two_ref, *refs):
    outs, acc = refs[skip:-1], refs[-1]
    width = first_ref.shape[0]
    acc[...] = first_ref[...] + contract_rows(one_ref[:, :width], one_ref[:, width:])
    acc[...] = acc[...] + contract_rows(two_ref[:, :width], two_ref[:, width:])

    rows = width // nz
    z, side = place_ref[0], place_ref[1]
    halves = len(outs) // 2
    cols = acc.shape[1] // halves

    def block(k, h):
        at = lax.rem(z + k * side + nz, nz)
        return acc[pl.ds(pl.multiple_of(at * rows, 16), rows), h * cols : (h + 1) * cols]

    for h in range(halves):
        kept, given = outs[2 * h : 2 * h + 2]
        for j in range(nz // 2):
            kept[j] = block(j, h)
            given[j] = block(-1 - j, h).astype(BF16)


def grad_terms(place, first, one, two, nz, halves, after):
    width, cols = first.shape
    shape = (nz // 2, width // nz, cols // halves)
    return pl.pallas_call(
        functools.partial(grad_kernel, nz, len(after)),
        out_shape=[jax.ShapeDtypeStruct(shape, F32), jax.ShapeDtypeStruct(shape, BF16)] * halves,
        in_specs=[SMEM] + [VMEM] * 3 + [pl.BlockSpec(memory_space=pl.ANY)] * len(after),
        out_specs=[VMEM] * (2 * halves),
        scratch_shapes=[pltpu.VMEM((width, cols), F32)],
        compiler_params=BIG,
    )(place, first, one, two, *after)


def relay_kernel(kept_ref, got_ref, *rest):
    near_ref, far_ref = rest[-2:]
    for j in range(2):
        near_ref[j] = kept_ref[j] + got_ref[j].astype(F32)
        far_ref[j] = (kept_ref[j + 2] + got_ref[j + 2].astype(F32)).astype(BF16)


def relay(kept, got, after):
    shape = (2, *kept.shape[1:])
    return pl.pallas_call(
        relay_kernel,
        out_shape=[jax.ShapeDtypeStruct(shape, F32), jax.ShapeDtypeStruct(shape, BF16)],
        in_specs=[VMEM] * 2 + [pl.BlockSpec(memory_space=pl.ANY)] * len(after),
        out_specs=[VMEM] * 2,
        compiler_params=PARAMS,
    )(kept, got, *after)


def project_first_kernel(y_ref, own_ref, both_ref, weight_ref, total_ref, out_ref):
    width = own_ref.shape[1]
    total_ref[...] = jnp.dot(own_ref[...], weight_ref[...], preferred_element_type=F32)
    out_ref[...] = jnp.dot(both_ref[:, :width], weight_ref[...], preferred_element_type=F32).astype(BF16)


def project_first(y, tokens, both, weight, ny):
    shape = (tokens.shape[0], weight.shape[1])
    return pl.pallas_call(
        project_first_kernel,
        out_shape=[jax.ShapeDtypeStruct(shape, F32), jax.ShapeDtypeStruct(shape, BF16)],
        grid_spec=pltpu.PrefetchScalarGridSpec(
            num_scalar_prefetch=1,
            grid=(1,),
            in_specs=[own_columns(tokens, ny), whole(both), whole(weight)],
            out_specs=[pl.BlockSpec(shape, lambda i, y: (0, 0))] * 2,
        ),
        compiler_params=BIG,
    )(y, tokens, both, weight)


def project_kernel(one_ref, two_ref, weight_ref, one_out, two_out):
    width = weight_ref.shape[0]
    for both, out in ((one_ref, one_out), (two_ref, two_out)):
        out[...] = jnp.dot(both[:, :width], weight_ref[...], preferred_element_type=F32).astype(BF16)


def project_rest(one, two, weight):
    shape = jax.ShapeDtypeStruct((one.shape[0], weight.shape[1]), BF16)
    return pl.pallas_call(
        project_kernel,
        out_shape=[shape, shape],
        in_specs=[VMEM] * 3,
        out_specs=[VMEM] * 2,
        compiler_params=PARAMS,
    )(one, two, weight)


def keep_kernel(kept_ref, keep_ref):
    kept = kept_ref[...].astype(F32).astype(BF16)
    rows, lanes = keep_ref.shape
    freq = lax.rem(lax.broadcasted_iota(jnp.int32, (rows, lanes), 1), FREQ).astype(F32)
    slot = lax.broadcasted_iota(jnp.int32, (kept.shape[1], lanes), 0)
    first = lax.broadcasted_iota(jnp.int32, (kept.shape[1], lanes), 1) // FREQ * TOPK
    keep = jnp.zeros((rows, lanes), F32)
    for j in range(TOPK):
        spread = (slot == first + j).astype(F32).astype(BF16)
        index = jnp.dot(kept, spread, preferred_element_type=F32)
        keep = jnp.where(index == freq, 1.0, keep)
    keep_ref[...] = keep


def keep_mask(kept_index):
    rows, slots = kept_index.shape
    return pl.pallas_call(
        keep_kernel,
        out_shape=jax.ShapeDtypeStruct((rows, slots // TOPK * FREQ), F32),
        in_specs=[VMEM],
        out_specs=VMEM,
        compiler_params=PARAMS,
    )(kept_index)


def encode_kernel(start, momentum_ref, keep_ref, table_ref, near_ref, far_ref, last_ref, *rest):
    blended_ref, coeff_ref, sent_ref = rest[-3:]
    for g in range(blended_ref.shape[1] // GROUP):
        cols = slice(g * GROUP, (g + 1) * GROUP)
        lanes = slice(g * 128, (g + 1) * 128)
        at = start + g * GROUP
        grad = near_ref[0, :, cols] + far_ref[0, :, cols].astype(F32) + last_ref[:, cols].astype(F32)
        blended = 0.9 * momentum_ref[:, at : at + GROUP] + grad
        coeffs = jnp.dot(blended, table_ref[...], precision=HIGHEST, preferred_element_type=F32)
        at = at // GROUP * 128
        coeffs = coeffs * keep_ref[:, at : at + 128]
        blended_ref[:, cols] = blended
        coeff_ref[:, lanes] = coeffs
        sent_ref[:, lanes] = coeffs.astype(BF16)


def encode(start, momentum, keep, table, grads, after):
    rows, cols = grads[2].shape
    lanes = cols // GROUP * 128
    return pl.pallas_call(
        functools.partial(encode_kernel, start),
        out_shape=[
            jax.ShapeDtypeStruct((rows, cols), F32),
            jax.ShapeDtypeStruct((rows, lanes), F32),
            jax.ShapeDtypeStruct((rows, lanes), BF16),
        ],
        in_specs=[VMEM] * (3 + len(grads)) + [pl.BlockSpec(memory_space=pl.ANY)] * len(after),
        out_specs=[VMEM] * 3,
        compiler_params=PARAMS,
    )(momentum, keep, table, *grads, *after)


def subtract_kernel(table_t_ref, *refs):
    new_ref = refs[-1]
    at = 0
    for blended_ref, coeff_ref in zip(refs[:-1:2], refs[1:-1:2]):
        for g in range(blended_ref.shape[1] // GROUP):
            new_ref[:, at : at + GROUP] = blended_ref[:, g * GROUP : (g + 1) * GROUP] - jnp.dot(
                coeff_ref[:, g * 128 : (g + 1) * 128],
                table_t_ref[...],
                precision=HIGHEST,
                preferred_element_type=F32,
            )
            at += GROUP


def subtract_rebuilt(table, parts, shape):
    return pl.pallas_call(
        subtract_kernel,
        out_shape=jax.ShapeDtypeStruct(shape, F32),
        in_specs=[VMEM] * (1 + len(parts)),
        out_specs=VMEM,
        compiler_params=PARAMS,
    )(table.T, *parts)


def combine_kernel(count, *refs):
    total_ref = refs[-1]
    at = 0
    for i in range(0, 4 * count, 4):
        own, one, two, three = (ref[...].astype(F32) for ref in refs[i : i + 4])
        total_ref[:, at : at + own.shape[1]] = (own + one) + (two + three)
        at += own.shape[1]


def combine(parts, after):
    count = len(parts) // 4
    rows = parts[0].shape[0]
    lanes = sum(part.shape[1] for part in parts[::4])
    return pl.pallas_call(
        functools.partial(combine_kernel, count),
        out_shape=jax.ShapeDtypeStruct((rows, lanes), F32),
        in_specs=[VMEM] * len(parts) + [pl.BlockSpec(memory_space=pl.ANY)] * len(after),
        out_specs=VMEM,
        compiler_params=PARAMS,
    )(*parts, *after)


def decode_kernel(mine_ref, other_ref, table_t_ref, update_ref):
    for g in range(update_ref.shape[1] // GROUP):
        lanes = slice(g * 128, (g + 1) * 128)
        coeffs = mine_ref[:, lanes] + other_ref[:, lanes]
        update_ref[:, g * GROUP : (g + 1) * GROUP] = jnp.dot(
            coeffs, table_t_ref[...], precision=HIGHEST, preferred_element_type=F32
        )


def decode(mine, other, table, width):
    return pl.pallas_call(
        decode_kernel,
        out_shape=jax.ShapeDtypeStruct((mine.shape[0], width), F32),
        in_specs=[VMEM] * 3,
        out_specs=VMEM,
        compiler_params=PARAMS,
    )(mine, other, table.T)


def swap(array, axis, d):
    return lax.ppermute(array, axis, [(i, i ^ d) for i in range(lax.axis_size(axis))])


def sides(nz):
    return [(c, z, 1 if (z + c) % 2 else -1) for c in range(2) for z in range(nz)]


def move(array, steps):
    nz = lax.axis_size("z")
    return lax.ppermute(array, ("core", "z"), [(c * nz + z, c * nz + (z + steps * side) % nz) for c, z, side in sides(nz)])


def reduce_over_z(kept, given, after):
    near, far = relay(kept, move(given, -1), after)
    far = move(far, 2)
    last = move((near[1] + far[1].astype(F32)).astype(BF16), 1)
    return [near, far, last]


def per_device(tokens, cotangent, weight, momentum, lengths, kept_index):
    ny, nz = lax.axis_size("y"), lax.axis_size("z")
    y = lax.axis_index("y").astype(jnp.int32).reshape(1)
    z = lax.axis_index("z").astype(jnp.int32)
    place = jnp.stack([z, 2 * ((z + lax.axis_index("core").astype(jnp.int32)) % 2) - 1])
    width = weight.shape[1]

    weight_quarter = lax.all_gather(weight, "z", axis=0, tiled=True)
    sent_two, sent_one, sent_three = split_inputs(y, lengths, tokens, cotangent, ny, (2, 1, 3))
    two = swap(sent_two, "y", 2)
    one, three = swap(sent_one, "y", 1), swap(sent_three, "y", 3)

    total, back_two = project_first(y, tokens, two, weight_quarter, ny)
    first = grad_first(y, lengths, tokens, cotangent, two, ny, weight_quarter)
    keep = keep_mask(kept_index)
    terms = grad_terms(place, first, one, three, nz, HALVES, (back_two, keep))
    back_one, back_three = project_rest(one, three, weight_quarter)
    backs = [swap(back_two, "y", 2), swap(back_one, "y", 1), swap(back_three, "y", 3)]

    table = group_table()
    sums, blends = [], []
    for h in range(HALVES):
        grads = reduce_over_z(*terms[2 * h : 2 * h + 2], (back_one, back_three, *backs[: 1 - h]))
        after = backs[1:] if h == HALVES - 1 else ()
        blended, coeffs, sent = encode(h * width // HALVES, momentum[0], keep, table, grads, after)
        blends += [blended, coeffs]
        sums += [sent] + [swap(sent, "x", d) for d in (1, 2, 3)]

    projected = (total + sum(back.astype(F32) for back in backs)).astype(BF16)
    new_momentum = subtract_rebuilt(table, blends, momentum.shape[1:])
    mine = combine(sums, (projected, new_momentum))
    update = decode(mine, swap(mine, "core", 1), table, width)
    return (projected, new_momentum[None], update)


def solution(mesh):
    fine = Mesh(mesh.devices.reshape(4, 2, 4, 8), ("x", "core", "y", "z"))
    rep, fsdp = ("x", "core"), ("y", "z")
    placed = (
        P(rep + fsdp, None),
        P(rep + fsdp, None),
        P(fsdp, None),
        P(rep, fsdp, None),
        P(rep + fsdp),
        P(fsdp, None),
    )
    return jax.shard_map(
        per_device,
        mesh=fine,
        in_specs=placed,
        out_specs=(P(rep + fsdp, None), P(rep, fsdp, None), P(fsdp, None)),
        check_vma=False,
    )
```

profile of v0, /device:TPU:1, one launch (start us, length us, event | category | flops | bytes accessed | tf_op | source)
XLA Modules:
  0.0 130.9 jit_solution(14158062077516630024)
XLA Ops:
  8.6 3.2 %shard_map.94 = (bf16[256,2176]{1,0:T(8,128)(2,1)}, bf16[256,2176]{1,0:T(8,128)(2,1)}, bf16[256,2176]{1,0:T(8,128)(2,1)}) custom-call(s32[1]{0:T(128)} %bitcast.y_ref, s32[1]{0:T(128)S(6)} %copy.10.length_ref, bf16[256,4608]{1,0:T(8,128)(2,1)} %own_ref.3, bf16[256,1024]{1,0:T(8,128)(2,1)} %cot_ref.3), custom_call_target="tpu_custom_call" | custom-call | tf_op jit(solution)/shard_map/pallas_call | solution.py:70
  11.8 3.8 %collective-permute-start = (bf16[256,2176]{1,0:T(8,128)(2,1)}, bf16[256,2176]{1,0:T(8,128)(2,1)}, u32[]{:S(2)}, u32[]{:S(2)}) collective-permute-start(bf16[256,2176]{1,0:T(8,128)(2,1)} %get-tuple-element.24), channel_id=1, source_target_pairs={{0,16},{8,24},{16,0},{24,8},{1,17},{9,25},{17,1},{25,9},{2,18},{10... | collective-permute-start | bytes 3342344 | tf_op jit(solution)/shard_map/ppermute | solution.py:337
  17.9 21.3 %collective-permute-done.both_ref = bf16[256,2176]{1,0:T(8,128)(2,1)} collective-permute-done((bf16[256,2176]{1,0:T(8,128)(2,1)}, bf16[256,2176]{1,0:T(8,128)(2,1)}, u32[]{:S(2)}, u32[]{:S(2)}) %collective-permute-start) | collective-permute-done | bytes 1114144 | tf_op jit(solution)/shard_map/ppermute | solution.py:337
  39.2 13.0 %all-gather.2.cloned.1.call-done.weight_ref.after_ref = bf16[1152,1024]{1,0:T(8,128)(2,1)} async-done(((bf16[144,1024]{1,0:T(8,128)(2,1)}), bf16[1152,1024]{1,0:T(8,128)(2,1)}) %all-gather.2.cloned.1.call-update) | async-done | bytes 2359312 | tf_op jit(solution)/shard_map/all_gather | solution.py:363
  52.3 1.7 %copy-done.1 = bf16[1152,1024]{1,0:T(8,128)(2,1)S(1)} copy-done((bf16[1152,1024]{1,0:T(8,128)(2,1)S(1)}, bf16[1152,1024]{1,0:T(8,128)(2,1)}, u32[]{:S(2)}) %copy-start.1) | copy-done | bytes 2359320
  53.9 2.9 %shard_map.95 = (f32[256,1024]{1,0:T(8,128)S(1)}, bf16[256,1024]{1,0:T(8,128)(2,1)S(1)}) custom-call(s32[1]{0:T(128)} %bitcast.y_ref, bf16[256,4608]{1,0:T(8,128)(2,1)S(1)} %copy-done, bf16[256,2176]{1,0:T(8,128)(2,1)} %collective-permute-done.both_ref, bf16[1152,1024]{1,0:T(8,128)(2,1)S(1)} %copy-done.1), custom_call_target="tpu_custom_call" | custom-call | tf_op jit(solution)/shard_map/pallas_call | solution.py:184
  56.8 2.7 %shard_map.98.first_ref = f32[1152,1024]{1,0:T(8,128)S(1)} custom-call(s32[1]{0:T(128)} %bitcast.y_ref, s32[1]{0:T(128)S(6)} %copy.10.length_ref, bf16[256,4608]{1,0:T(8,128)(2,1)S(1)} %copy-done, bf16[256,1024]{1,0:T(8,128)(2,1)S(1)} %copy-done.5, bf16[256,2176]{1,0:T(8,128)(2,1)} %collective-permute-done.both_ref, bf16[1152,1024]{1,0:T(8,128)(2,1)S(1)} %copy-done.1), custom_call_target="tpu_custom_call" | custom-call | tf_op jit(solution)/shard_map/pallas_call | solution.py:105
  59.5 4.7 %collective-permute-done.2.one_ref = bf16[256,2176]{1,0:T(8,128)(2,1)} collective-permute-done((bf16[256,2176]{1,0:T(8,128)(2,1)}, bf16[256,2176]{1,0:T(8,128)(2,1)}, u32[]{:S(2)}, u32[]{:S(2)}) %collective-permute-start.2) | collective-permute-done | bytes 1114144 | tf_op jit(solution)/shard_map/ppermute | solution.py:337
  64.8 3.5 %shard_map.99 = (f32[4,144,512]{2,1,0:T(8,128)S(1)}, bf16[4,144,512]{2,1,0:T(8,128)(2,1)S(1)}, f32[4,144,512]{2,1,0:T(8,128)S(1)}, bf16[4,144,512]{2,1,0:T(8,128)(2,1)S(1)}) custom-call(s32[2]{0:T(128)S(1)} %pad_add_fusion.place_ref, f32[1152,1024]{1,0:T(8,128)S(1)} %shard_map.98.first_ref, bf16[256,2176]{1,0:T(8,128)(2,1)} %collective-permute-done.2.one_ref, ...), custom_call_target="tpu_custom_call" | custom-call | tf_op jit(solution)/shard_map/pallas_call | solution.py:148
  68.3 5.7 %collective-permute-start.6 = (bf16[4,144,512]{2,1,0:T(8,128)(2,1)S(1)}, bf16[4,144,512]{2,1,0:T(8,128)(2,1)S(1)}, u32[]{:S(2)}, u32[]{:S(2)}) collective-permute-start(bf16[4,144,512]{2,1,0:T(8,128)(2,1)S(1)} %get-tuple-element.32), channel_id=1, source_target_pairs={{0,1},{1,0},{2,3},{3,2},{4,5},{5,4},{6,7},{7,6},{32,39},{33,34},{3... | collective-permute-start | bytes 1769480 | tf_op jit(solution)/shard_map/ppermute | solution.py:346
  74.0 2.9 %collective-permute-start.1 = (bf16[256,1024]{1,0:T(8,128)(2,1)S(1)}, bf16[256,1024]{1,0:T(8,128)(2,1)S(1)}, u32[]{:S(2)}, u32[]{:S(2)}) collective-permute-start(bf16[256,1024]{1,0:T(8,128)(2,1)S(1)} %get-tuple-element.26.refs_0_), channel_id=1, source_target_pairs={{0,16},{8,24},{16,0},{24,8},{1,17},{9,25},{17,1},{25,9},{2,18},{10... | collective-permute-start | bytes 1572872 | tf_op jit(solution)/shard_map/ppermute | solution.py:337
  77.0 3.1 %shard_map.96 = (bf16[256,1024]{1,0:T(8,128)(2,1)S(1)}, bf16[256,1024]{1,0:T(8,128)(2,1)S(1)}) custom-call(bf16[256,2176]{1,0:T(8,128)(2,1)} %collective-permute-done.2.one_ref, bf16[256,2176]{1,0:T(8,128)(2,1)} %collective-permute-done.3.two_ref, bf16[1152,1024]{1,0:T(8,128)(2,1)S(1)} %copy-done.2), custom_call_target="tpu_custom_call" | custom-call | tf_op jit(solution)/shard_map/pallas_call | solution.py:205
  80.2 6.7 %collective-permute-done.1.rest_2_ = bf16[256,1024]{1,0:T(8,128)(2,1)S(1)} collective-permute-done((bf16[256,1024]{1,0:T(8,128)(2,1)S(1)}, bf16[256,1024]{1,0:T(8,128)(2,1)S(1)}, u32[]{:S(2)}, u32[]{:S(2)}) %collective-permute-start.1) | collective-permute-done | bytes 524320 | tf_op jit(solution)/shard_map/ppermute | solution.py:337
  87.7 1.5 %collective-permute-start.10 = (bf16[2,144,512]{2,1,0:T(8,128)(2,1)S(1)}, bf16[2,144,512]{2,1,0:T(8,128)(2,1)S(1)}, u32[]{:S(2)}, u32[]{:S(2)}) collective-permute-start(bf16[2,144,512]{2,1,0:T(8,128)(2,1)S(1)} %get-tuple-element.40), channel_id=1, source_target_pairs={{0,6},{1,3},{2,0},{3,5},{4,2},{5,7},{6,4},{7,1},{32,34},{33,39},{3... | collective-permute-start | bytes 884744 | tf_op jit(solution)/shard_map/ppermute | solution.py:346
  89.2 1.5 %collective-permute-start.4 = (bf16[256,1024]{1,0:T(8,128)(2,1)S(1)}, bf16[256,1024]{1,0:T(8,128)(2,1)S(1)}, u32[]{:S(2)}, u32[]{:S(2)}) collective-permute-start(bf16[256,1024]{1,0:T(8,128)(2,1)S(1)} %get-tuple-element.29.rest_0_), channel_id=1, source_target_pairs={{0,8},{8,0},{16,24},{24,16},{1,9},{9,1},{17,25},{25,17},{2,10},{10... | collective-permute-start | bytes 1572872 | tf_op jit(solution)/shard_map/ppermute | solution.py:337
  90.8 2.1 %collective-permute-start.5 = (bf16[256,1024]{1,0:T(8,128)(2,1)S(1)}, bf16[256,1024]{1,0:T(8,128)(2,1)S(1)}, u32[]{:S(2)}, u32[]{:S(2)}) collective-permute-start(bf16[256,1024]{1,0:T(8,128)(2,1)S(1)} %get-tuple-element.30.rest_1_), channel_id=1, source_target_pairs={{0,24},{8,16},{16,8},{24,0},{1,25},{9,17},{17,9},{25,1},{2,26},{10... | collective-permute-start | bytes 1572872 | tf_op jit(solution)/shard_map/ppermute | solution.py:337
  92.8 2.0 %collective-permute-done.7.far_ref = bf16[2,144,512]{2,1,0:T(8,128)(2,1)S(1)} collective-permute-done((bf16[2,144,512]{2,1,0:T(8,128)(2,1)S(1)}, bf16[2,144,512]{2,1,0:T(8,128)(2,1)S(1)}, u32[]{:S(2)}, u32[]{:S(2)}) %collective-permute-start.7) | collective-permute-done | bytes 294944 | tf_op jit(solution)/shard_map/ppermute | solution.py:346
  95.8 2.6 %collective-permute-done.10.far_ref = bf16[2,144,512]{2,1,0:T(8,128)(2,1)S(1)} collective-permute-done((bf16[2,144,512]{2,1,0:T(8,128)(2,1)S(1)}, bf16[2,144,512]{2,1,0:T(8,128)(2,1)S(1)}, u32[]{:S(2)}, u32[]{:S(2)}) %collective-permute-start.10) | collective-permute-done | bytes 294944 | tf_op jit(solution)/shard_map/ppermute | solution.py:346
  98.4 2.0 %collective-permute-start.11 = (bf16[144,512]{1,0:T(8,128)(2,1)S(1)}, bf16[144,512]{1,0:T(8,128)(2,1)S(1)}, u32[]{:S(2)}, u32[]{:S(2)}) collective-permute-start(bf16[144,512]{1,0:T(8,128)(2,1)S(1)} %fusion.1), channel_id=1, source_target_pairs={{0,7},{1,2},{2,1},{3,4},{4,3},{5,6},{6,5},{7,0},{32,33},{33,32},{3... | collective-permute-start | bytes 442376 | tf_op jit(solution)/shard_map/ppermute | solution.py:346
  100.4 3.2 %collective-permute-done.8.last_ref = bf16[144,512]{1,0:T(8,128)(2,1)S(1)} collective-permute-done((bf16[144,512]{1,0:T(8,128)(2,1)S(1)}, bf16[144,512]{1,0:T(8,128)(2,1)S(1)}, u32[]{:S(2)}, u32[]{:S(2)}) %collective-permute-start.8) | collective-permute-done | bytes 147488 | tf_op jit(solution)/shard_map/ppermute | solution.py:346
  104.1 2.6 %collective-permute-start.14 = (bf16[144,256]{1,0:T(8,128)(2,1)S(1)}, bf16[144,256]{1,0:T(8,128)(2,1)S(1)}, u32[]{:S(2)}, u32[]{:S(2)}) collective-permute-start(bf16[144,256]{1,0:T(8,128)(2,1)S(1)} %get-tuple-element.43.refs_0_), channel_id=1, source_target_pairs={{0,192},{64,128},{128,64},{192,0},{1,193},{65,129},{129,65},{193,1... | collective-permute-start | bytes 221192 | tf_op jit(solution)/shard_map/ppermute | solution.py:337
  108.0 2.6 %collective-permute-start.17 = (bf16[144,256]{1,0:T(8,128)(2,1)S(1)}, bf16[144,256]{1,0:T(8,128)(2,1)S(1)}, u32[]{:S(2)}, u32[]{:S(2)}) collective-permute-start(bf16[144,256]{1,0:T(8,128)(2,1)S(1)} %get-tuple-element.44.refs_4_), channel_id=1, source_target_pairs={{0,192},{64,128},{128,64},{192,0},{1,193},{65,129},{129,65},{193,1... | collective-permute-start | bytes 221192 | tf_op jit(solution)/shard_map/ppermute | solution.py:337
  113.6 2.3 %collective-permute-done.16.refs_6_ = bf16[144,256]{1,0:T(8,128)(2,1)S(1)} collective-permute-done((bf16[144,256]{1,0:T(8,128)(2,1)S(1)}, bf16[144,256]{1,0:T(8,128)(2,1)S(1)}, u32[]{:S(2)}, u32[]{:S(2)}) %collective-permute-start.16) | collective-permute-done | bytes 73760 | tf_op jit(solution)/shard_map/ppermute | solution.py:337
  117.1 4.3 %collective-permute-start.18 = (f32[144,512]{1,0:T(8,128)S(1)}, f32[144,512]{1,0:T(8,128)S(1)}, u32[]{:S(2)}, u32[]{:S(2)}) collective-permute-start(f32[144,512]{1,0:T(8,128)S(1)} %shard_map.105.mine_ref), channel_id=1, source_target_pairs={{0,32},{32,0},{1,33},{33,1},{2,34},{34,2},{3,35},{35,3},{4,36},{36... | collective-permute-start | bytes 884744 | tf_op jit(solution)/shard_map/ppermute | solution.py:337
  (54 shorter events, 14.1 us)
Async XLA Ops:
  7.2 45.1 %all-gather.2.cloned.1.call-start = ((), (), s32[]{:S(2)}) async-start(), calls=%async_computation | async-start | bytes 2654208 | tf_op jit(solution)/shard_map/all_gather | solution.py:363
  8.6 43.7 %copy-start = (bf16[256,4608]{1,0:T(8,128)(2,1)S(1)}, bf16[256,4608]{1,0:T(8,128)(2,1)}, u32[]{:S(2)}) copy-start(bf16[256,4608]{1,0:T(8,128)(2,1)} %own_ref.3) | copy-start | bytes 7077892
  11.8 27.4 %collective-permute-start = (bf16[256,2176]{1,0:T(8,128)(2,1)}, bf16[256,2176]{1,0:T(8,128)(2,1)}, u32[]{:S(2)}, u32[]{:S(2)}) collective-permute-start(bf16[256,2176]{1,0:T(8,128)(2,1)} %get-tuple-element.24), channel_id=1, source_target_pairs={{0,16},{8,24},{16,0},{24,8},{1,17},{9,25},{17,1},{25,9},{2,18},{10... | collective-permute-start | bytes 3342344 | tf_op jit(solution)/shard_map/ppermute | solution.py:337
  15.6 48.6 %collective-permute-start.2 = (bf16[256,2176]{1,0:T(8,128)(2,1)}, bf16[256,2176]{1,0:T(8,128)(2,1)}, u32[]{:S(2)}, u32[]{:S(2)}) collective-permute-start(bf16[256,2176]{1,0:T(8,128)(2,1)} %get-tuple-element.27), channel_id=1, source_target_pairs={{0,8},{8,0},{16,24},{24,16},{1,9},{9,1},{17,25},{25,17},{2,10},{10... | collective-permute-start | bytes 3342344 | tf_op jit(solution)/shard_map/ppermute | solution.py:337
  16.0 48.8 %collective-permute-start.3 = (bf16[256,2176]{1,0:T(8,128)(2,1)}, bf16[256,2176]{1,0:T(8,128)(2,1)}, u32[]{:S(2)}, u32[]{:S(2)}) collective-permute-start(bf16[256,2176]{1,0:T(8,128)(2,1)} %get-tuple-element.28), channel_id=1, source_target_pairs={{0,24},{8,16},{16,8},{24,0},{1,25},{9,17},{17,9},{25,1},{2,26},{10... | collective-permute-start | bytes 3342344 | tf_op jit(solution)/shard_map/ppermute | solution.py:337
  64.8 12.2 %copy-start.2 = (bf16[1152,1024]{1,0:T(8,128)(2,1)S(1)}, bf16[1152,1024]{1,0:T(8,128)(2,1)}, u32[]{:S(2)}) copy-start(bf16[1152,1024]{1,0:T(8,128)(2,1)} %all-gather.2.cloned.1.call-done.weight_ref.after_ref) | copy-start | bytes 7077892
  68.3 18.6 %collective-permute-start.6 = (bf16[4,144,512]{2,1,0:T(8,128)(2,1)S(1)}, bf16[4,144,512]{2,1,0:T(8,128)(2,1)S(1)}, u32[]{:S(2)}, u32[]{:S(2)}) collective-permute-start(bf16[4,144,512]{2,1,0:T(8,128)(2,1)S(1)} %get-tuple-element.32), channel_id=1, source_target_pairs={{0,1},{1,0},{2,3},{3,2},{4,5},{5,4},{6,7},{7,6},{32,39},{33,34},{3... | collective-permute-start | bytes 1769480 | tf_op jit(solution)/shard_map/ppermute | solution.py:346
  74.0 12.8 %collective-permute-start.1 = (bf16[256,1024]{1,0:T(8,128)(2,1)S(1)}, bf16[256,1024]{1,0:T(8,128)(2,1)S(1)}, u32[]{:S(2)}, u32[]{:S(2)}) collective-permute-start(bf16[256,1024]{1,0:T(8,128)(2,1)S(1)} %get-tuple-element.26.refs_0_), channel_id=1, source_target_pairs={{0,16},{8,24},{16,0},{24,8},{1,17},{9,25},{17,1},{25,9},{2,18},{10... | collective-permute-start | bytes 1572872 | tf_op jit(solution)/shard_map/ppermute | solution.py:337
  76.9 10.7 %collective-permute-start.9 = (bf16[4,144,512]{2,1,0:T(8,128)(2,1)S(1)}, bf16[4,144,512]{2,1,0:T(8,128)(2,1)S(1)}, u32[]{:S(2)}, u32[]{:S(2)}) collective-permute-start(bf16[4,144,512]{2,1,0:T(8,128)(2,1)S(1)} %get-tuple-element.38), channel_id=1, source_target_pairs={{0,1},{1,0},{2,3},{3,2},{4,5},{5,4},{6,7},{7,6},{32,39},{33,34},{3... | collective-permute-start | bytes 1769480 | tf_op jit(solution)/shard_map/ppermute | solution.py:346
  87.0 7.9 %collective-permute-start.7 = (bf16[2,144,512]{2,1,0:T(8,128)(2,1)S(1)}, bf16[2,144,512]{2,1,0:T(8,128)(2,1)S(1)}, u32[]{:S(2)}, u32[]{:S(2)}) collective-permute-start(bf16[2,144,512]{2,1,0:T(8,128)(2,1)S(1)} %get-tuple-element.34), channel_id=1, source_target_pairs={{0,6},{1,3},{2,0},{3,5},{4,2},{5,7},{6,4},{7,1},{32,34},{33,39},{3... | collective-permute-start | bytes 884744 | tf_op jit(solution)/shard_map/ppermute | solution.py:346
  87.7 16.0 %copy-start.4 = (f32[1,144,1024]{2,1,0:T(8,128)S(1)}, f32[1,144,1024]{2,1,0:T(8,128)}, u32[]{:S(2)}) copy-start(f32[1,144,1024]{2,1,0:T(8,128)} %param.10) | copy-start | bytes 1769476
  87.7 16.0 %copy-start.8 = (f32[256,128]{1,0:T(8,128)S(1)}, f32[256,128]{1,0:T(8,128)}, u32[]{:S(2)}) copy-start(f32[256,128]{1,0:T(8,128)} %constant.32.clone.table_ref) | copy-start | bytes 393220
  87.7 10.6 %collective-permute-start.10 = (bf16[2,144,512]{2,1,0:T(8,128)(2,1)S(1)}, bf16[2,144,512]{2,1,0:T(8,128)(2,1)S(1)}, u32[]{:S(2)}, u32[]{:S(2)}) collective-permute-start(bf16[2,144,512]{2,1,0:T(8,128)(2,1)S(1)} %get-tuple-element.40), channel_id=1, source_target_pairs={{0,6},{1,3},{2,0},{3,5},{4,2},{5,7},{6,4},{7,1},{32,34},{33,39},{3... | collective-permute-start | bytes 884744 | tf_op jit(solution)/shard_map/ppermute | solution.py:346
  89.2 18.0 %collective-permute-start.4 = (bf16[256,1024]{1,0:T(8,128)(2,1)S(1)}, bf16[256,1024]{1,0:T(8,128)(2,1)S(1)}, u32[]{:S(2)}, u32[]{:S(2)}) collective-permute-start(bf16[256,1024]{1,0:T(8,128)(2,1)S(1)} %get-tuple-element.29.rest_0_), channel_id=1, source_target_pairs={{0,8},{8,0},{16,24},{24,16},{1,9},{9,1},{17,25},{25,17},{2,10},{10... | collective-permute-start | bytes 1572872 | tf_op jit(solution)/shard_map/ppermute | solution.py:337
  90.8 16.7 %collective-permute-start.5 = (bf16[256,1024]{1,0:T(8,128)(2,1)S(1)}, bf16[256,1024]{1,0:T(8,128)(2,1)S(1)}, u32[]{:S(2)}, u32[]{:S(2)}) collective-permute-start(bf16[256,1024]{1,0:T(8,128)(2,1)S(1)} %get-tuple-element.30.rest_1_), channel_id=1, source_target_pairs={{0,24},{8,16},{16,8},{24,0},{1,25},{9,17},{17,9},{25,1},{2,26},{10... | collective-permute-start | bytes 1572872 | tf_op jit(solution)/shard_map/ppermute | solution.py:337
  94.9 8.8 %collective-permute-start.8 = (bf16[144,512]{1,0:T(8,128)(2,1)S(1)}, bf16[144,512]{1,0:T(8,128)(2,1)S(1)}, u32[]{:S(2)}, u32[]{:S(2)}) collective-permute-start(bf16[144,512]{1,0:T(8,128)(2,1)S(1)} %fusion), channel_id=1, source_target_pairs={{0,7},{1,2},{2,1},{3,4},{4,3},{5,6},{6,5},{7,0},{32,33},{33,32},{3... | collective-permute-start | bytes 442376 | tf_op jit(solution)/shard_map/ppermute | solution.py:346
  98.4 9.1 %collective-permute-start.11 = (bf16[144,512]{1,0:T(8,128)(2,1)S(1)}, bf16[144,512]{1,0:T(8,128)(2,1)S(1)}, u32[]{:S(2)}, u32[]{:S(2)}) collective-permute-start(bf16[144,512]{1,0:T(8,128)(2,1)S(1)} %fusion.1), channel_id=1, source_target_pairs={{0,7},{1,2},{2,1},{3,4},{4,3},{5,6},{6,5},{7,0},{32,33},{33,32},{3... | collective-permute-start | bytes 442376 | tf_op jit(solution)/shard_map/ppermute | solution.py:346
  104.1 6.9 %collective-permute-start.14 = (bf16[144,256]{1,0:T(8,128)(2,1)S(1)}, bf16[144,256]{1,0:T(8,128)(2,1)S(1)}, u32[]{:S(2)}, u32[]{:S(2)}) collective-permute-start(bf16[144,256]{1,0:T(8,128)(2,1)S(1)} %get-tuple-element.43.refs_0_), channel_id=1, source_target_pairs={{0,192},{64,128},{128,64},{192,0},{1,193},{65,129},{129,65},{193,1... | collective-permute-start | bytes 221192 | tf_op jit(solution)/shard_map/ppermute | solution.py:337
  106.7 6.9 %collective-permute-start.13 = (bf16[144,256]{1,0:T(8,128)(2,1)S(1)}, bf16[144,256]{1,0:T(8,128)(2,1)S(1)}, u32[]{:S(2)}, u32[]{:S(2)}) collective-permute-start(bf16[144,256]{1,0:T(8,128)(2,1)S(1)} %get-tuple-element.43.refs_0_), channel_id=1, source_target_pairs={{0,128},{64,192},{128,0},{192,64},{1,129},{65,193},{129,1},{193,65... | collective-permute-start | bytes 221192 | tf_op jit(solution)/shard_map/ppermute | solution.py:337
  107.2 6.4 %collective-permute-start.12 = (bf16[144,256]{1,0:T(8,128)(2,1)S(1)}, bf16[144,256]{1,0:T(8,128)(2,1)S(1)}, u32[]{:S(2)}, u32[]{:S(2)}) collective-permute-start(bf16[144,256]{1,0:T(8,128)(2,1)S(1)} %get-tuple-element.43.refs_0_), channel_id=1, source_target_pairs={{0,64},{64,0},{128,192},{192,128},{1,65},{65,1},{129,193},{193,129... | collective-permute-start | bytes 221192 | tf_op jit(solution)/shard_map/ppermute | solution.py:337
  108.0 5.7 %collective-permute-start.17 = (bf16[144,256]{1,0:T(8,128)(2,1)S(1)}, bf16[144,256]{1,0:T(8,128)(2,1)S(1)}, u32[]{:S(2)}, u32[]{:S(2)}) collective-permute-start(bf16[144,256]{1,0:T(8,128)(2,1)S(1)} %get-tuple-element.44.refs_4_), channel_id=1, source_target_pairs={{0,192},{64,128},{128,64},{192,0},{1,193},{65,129},{129,65},{193,1... | collective-permute-start | bytes 221192 | tf_op jit(solution)/shard_map/ppermute | solution.py:337
  110.5 5.4 %collective-permute-start.16 = (bf16[144,256]{1,0:T(8,128)(2,1)S(1)}, bf16[144,256]{1,0:T(8,128)(2,1)S(1)}, u32[]{:S(2)}, u32[]{:S(2)}) collective-permute-start(bf16[144,256]{1,0:T(8,128)(2,1)S(1)} %get-tuple-element.44.refs_4_), channel_id=1, source_target_pairs={{0,128},{64,192},{128,0},{192,64},{1,129},{65,193},{129,1},{193,65... | collective-permute-start | bytes 221192 | tf_op jit(solution)/shard_map/ppermute | solution.py:337
  111.0 4.9 %collective-permute-start.15 = (bf16[144,256]{1,0:T(8,128)(2,1)S(1)}, bf16[144,256]{1,0:T(8,128)(2,1)S(1)}, u32[]{:S(2)}, u32[]{:S(2)}) collective-permute-start(bf16[144,256]{1,0:T(8,128)(2,1)S(1)} %get-tuple-element.44.refs_4_), channel_id=1, source_target_pairs={{0,64},{64,0},{128,192},{192,128},{1,65},{65,1},{129,193},{193,129... | collective-permute-start | bytes 221192 | tf_op jit(solution)/shard_map/ppermute | solution.py:337
  117.1 5.5 %collective-permute-start.18 = (f32[144,512]{1,0:T(8,128)S(1)}, f32[144,512]{1,0:T(8,128)S(1)}, u32[]{:S(2)}, u32[]{:S(2)}) collective-permute-start(f32[144,512]{1,0:T(8,128)S(1)} %shard_map.105.mine_ref), channel_id=1, source_target_pairs={{0,32},{32,0},{1,33},{33,1},{2,34},{34,2},{3,35},{35,3},{4,36},{36... | collective-permute-start | bytes 884744 | tf_op jit(solution)/shard_map/ppermute | solution.py:337
  (6 other events, 19.8 us)
Sparse Core Ops, SparseCore 0:
  9.8 42.4 all-gather.1
where the time goes:
time: 131 us
  waiting for transfers between devices  58.9 us (45%)
  starting transfers between devices  32.4 us (25%)
  Pallas kernels  20.9 us (16%)
  between operations  14.8 us (11%)
  local copies, waits for them, and re-layouts  3.3 us (3%)
    ppermute x13, waiting for transfers between devices, swap(): lax.ppermute(array, axis, [(i, i ^ d) for i in range(lax.axis_size(axis))])  36.8 us
    ppermute x13, starting transfers between devices, swap(): lax.ppermute(array, axis, [(i, i ^ d) for i in range(lax.axis_size(axis))])  22.1 us
    all_gather x1, waiting for transfers between devices, per_device(): weight_quarter = lax.all_gather(weight, 'z', axis=0, tiled=True)  13 us
    ppermute x6, starting transfers between devices, move(): lax.ppermute(array, ('core', 'z'), [(c * nz + z, c * nz + (z + steps * si...  10.3 us
    ppermute x6, waiting for transfers between devices, move(): lax.ppermute(array, ('core', 'z'), [(c * nz + z, c * nz + (z + steps * si...  8.42 us
    pallas_call x1, Pallas kernels, grad_terms(): pl.pallas_call(functools.partial(grad_kernel, nz, len(after)), out_shape=...  3.45 us
    unnamed x20, local copies, waits for them, and re-layouts  3.3 us
    pallas_call x1, Pallas kernels, split_inputs(): pl.pallas_call(functools.partial(split_kernel, order), out_shape=[jax.Sha...  3.21 us
  transfers between devices with their start and end apart: 20, of which 11 were waited for; matrix products, arithmetic and copies ran while one was open for 0% of the time, Pallas kernels for 12%

commit v1 on v0

--- a/solution.py
+++ b/solution.py
@@ -19,6 +19,7 @@
 BF16 = jnp.bfloat16
 F32 = jnp.float32
 HIGHEST = lax.Precision.HIGHEST
+TOKEN = jax.ShapeDtypeStruct((8, 128), F32)
 VMEM = pl.BlockSpec(memory_space=pltpu.VMEM)
 SMEM = pl.BlockSpec(memory_space=pltpu.SMEM)
 HBM = pl.BlockSpec(memory_space=pltpu.HBM)
@@ -123,8 +124,8 @@
 def grad_kernel(nz, skip, place_ref, first_ref, one_ref, two_ref, *refs):
     outs, acc = refs[skip:-1], refs[-1]
     width = first_ref.shape[0]
-    acc[...] = first_ref[...] + contract_rows(one_ref[:, :width], one_ref[:, width:])
-    acc[...] = acc[...] + contract_rows(two_ref[:, :width], two_ref[:, width:])
+    both = jnp.concatenate([one_ref[...], two_ref[...]], axis=0)
+    acc[...] = first_ref[...] + contract_rows(both[:, :width], both[:, width:])
 
     rows = width // nz
     z, side = place_ref[0], place_ref[1]
@@ -269,9 +270,10 @@
 
 
 def subtract_kernel(table_t_ref, *refs):
-    new_ref = refs[-1]
+    parts, (new_ref, token_ref) = refs[:-2], refs[-2:]
+    token_ref[...] = jnp.zeros_like(token_ref)
     at = 0
-    for blended_ref, coeff_ref in zip(refs[:-1:2], refs[1:-1:2]):
+    for blended_ref, coeff_ref in zip(parts[::2], parts[1::2]):
         for g in range(blended_ref.shape[1] // GROUP):
             new_ref[:, at : at + GROUP] = blended_ref[:, g * GROUP : (g + 1) * GROUP] - jnp.dot(
                 coeff_ref[:, g * 128 : (g + 1) * 128],
@@ -285,11 +287,27 @@
 def subtract_rebuilt(table, parts, shape):
     return pl.pallas_call(
         subtract_kernel,
-        out_shape=jax.ShapeDtypeStruct(shape, F32),
+        out_shape=[jax.ShapeDtypeStruct(shape, F32), TOKEN],
         in_specs=[VMEM] * (1 + len(parts)),
-        out_specs=VMEM,
+        out_specs=[VMEM] * 2,
         compiler_params=PARAMS,
     )(table.T, *parts)
+
+
+def finish_kernel(total_ref, one_ref, two_ref, three_ref, out_ref, token_ref):
+    token_ref[...] = jnp.zeros_like(token_ref)
+    total = total_ref[...] + one_ref[...].astype(F32)
+    out_ref[...] = (total + (two_ref[...].astype(F32) + three_ref[...].astype(F32))).astype(BF16)
+
+
+def finish_projection(total, backs):
+    return pl.pallas_call(
+        finish_kernel,
+        out_shape=[jax.ShapeDtypeStruct(total.shape, BF16), TOKEN],
+        in_specs=[VMEM] * 4,
+        out_specs=[VMEM] * 2,
+        compiler_params=PARAMS,
+    )(total, *backs)
 
 
 def combine_kernel(count, *refs):
@@ -361,7 +379,8 @@
     width = weight.shape[1]
 
     weight_quarter = lax.all_gather(weight, "z", axis=0, tiled=True)
-    sent_two, sent_one, sent_three = split_inputs(y, lengths, tokens, cotangent, ny, (2, 1, 3))
+    (sent_two,) = split_inputs(y, lengths, tokens, cotangent, ny, (2,))
+    sent_one, sent_three = split_inputs(y, lengths, tokens, cotangent, ny, (1, 3))
     two = swap(sent_two, "y", 2)
     one, three = swap(sent_one, "y", 1), swap(sent_three, "y", 3)
 
@@ -375,15 +394,16 @@
     table = group_table()
     sums, blends = [], []
     for h in range(HALVES):
-        grads = reduce_over_z(*terms[2 * h : 2 * h + 2], (back_one, back_three, *backs[: 1 - h]))
-        after = backs[1:] if h == HALVES - 1 else ()
+        last = h == HALVES - 1
+        grads = reduce_over_z(*terms[2 * h : 2 * h + 2], (backs[0],) if last else (back_one, back_three))
+        after = backs[1:] if last else ()
         blended, coeffs, sent = encode(h * width // HALVES, momentum[0], keep, table, grads, after)
         blends += [blended, coeffs]
         sums += [sent] + [swap(sent, "x", d) for d in (1, 2, 3)]
 
-    projected = (total + sum(back.astype(F32) for back in backs)).astype(BF16)
-    new_momentum = subtract_rebuilt(table, blends, momentum.shape[1:])
-    mine = combine(sums, (projected, new_momentum))
+    projected, projected_token = finish_projection(total, backs)
+    new_momentum, new_token = subtract_rebuilt(table, blends, momentum.shape[1:])
+    mine = combine(sums, (projected_token, new_token))
     update = decode(mine, swap(mine, "core", 1), table, width)
     return (projected, new_momentum[None], update)
 

time: 131 us -> 130 us (level)
  waiting for transfers between devices: 58.9 us -> 54.5 us
  Pallas kernels: 20.9 us -> 23.6 us
  starting transfers between devices: 32.4 us -> 34.5 us
  local copies, waits for them, and re-layouts: 3.3 us -> 1.7 us
    ppermute x13, waiting for transfers between devices: 36.8 us -> 31.4 us  [swap(): lax.ppermute(array, axis, [(i, i ^ d) for i in range(lax.axis_size(axis))])]
    ppermute x6, starting transfers between devices: 10.3 us -> 12.6 us  [move(): lax.ppermute(array, ('core', 'z'), [(c * nz + z, c * nz + (z + steps * si...]
    pallas_call x1 -> x2, Pallas kernels: 3.21 us -> 4.97 us  [split_inputs(): pl.pallas_call(functools.partial(split_kernel, order), out_shape=[jax.Sha...]
    unnamed x20 -> x16, local copies, waits for them, and re-layouts: 3.3 us -> 1.7 us
  transfers between devices with their start and end apart: 20 -> 20, of which waited for: 11 -> 11; matrix products, arithmetic and copies ran while one was open for 0% -> 0% of each run, Pallas kernels for 12% -> 14%
where the time goes in v1:
time: 130 us; the launch traced here: 129 us
  waiting for transfers between devices  54.5 us (42%)
  starting transfers between devices  34.5 us (27%)
  Pallas kernels  23.6 us (18%)
  between operations  14.8 us (11%)
  local copies, waits for them, and re-layouts  1.7 us (1%)
    ppermute x13, waiting for transfers between devices, swap(): lax.ppermute(array, axis, [(i, i ^ d) for i in range(lax.axis_size(axis))])  31.4 us
    ppermute x13, starting transfers between devices, swap(): lax.ppermute(array, axis, [(i, i ^ d) for i in range(lax.axis_size(axis))])  21.8 us
    all_gather x1, waiting for transfers between devices, per_device(): weight_quarter = lax.all_gather(weight, 'z', axis=0, tiled=True)  13.9 us
    ppermute x6, starting transfers between devices, move(): lax.ppermute(array, ('core', 'z'), [(c * nz + z, c * nz + (z + steps * si...  12.6 us
    ppermute x6, waiting for transfers between devices, move(): lax.ppermute(array, ('core', 'z'), [(c * nz + z, c * nz + (z + steps * si...  8.51 us
    pallas_call x2, Pallas kernels, split_inputs(): pl.pallas_call(functools.partial(split_kernel, order), out_shape=[jax.Sha...  4.97 us
    pallas_call x1, Pallas kernels, grad_terms(): pl.pallas_call(functools.partial(grad_kernel, nz, len(after)), out_shape=...  3.43 us
    pallas_call x1, Pallas kernels, project_rest(): pl.pallas_call(project_kernel, out_shape=[shape, shape], in_specs=[VMEM]...  3.1 us
  transfers between devices with their start and end apart: 20, of which 11 were waited for; matrix products, arithmetic and copies ran while one was open for 0% of the time, Pallas kernels for 14%

profile of v1, /device:TPU:1, one launch (start us, length us, event | category | flops | bytes accessed | tf_op | source)
XLA Modules:
  0.0 129.3 jit_solution(3814078529599237494)
XLA Ops:
  8.5 2.3 %shard_map.94 = bf16[256,2176]{1,0:T(8,128)(2,1)} custom-call(s32[1]{0:T(128)} %bitcast.y_ref, s32[1]{0:T(128)S(6)} %copy.10.length_ref, bf16[256,4608]{1,0:T(8,128)(2,1)} %own_ref.3, bf16[256,1024]{1,0:T(8,128)(2,1)} %cot_ref.5), custom_call_target="tpu_custom_call" | custom-call | tf_op jit(solution)/shard_map/pallas_call | solution.py:71
  10.8 3.9 %collective-permute-start = (bf16[256,2176]{1,0:T(8,128)(2,1)}, bf16[256,2176]{1,0:T(8,128)(2,1)}, u32[]{:S(2)}, u32[]{:S(2)}) collective-permute-start(bf16[256,2176]{1,0:T(8,128)(2,1)} %shard_map.94), channel_id=1, source_target_pairs={{0,16},{8,24},{16,0},{24,8},{1,17},{9,25},{17,1},{25,9},{2,18},{10... | collective-permute-start | bytes 3342344 | tf_op jit(solution)/shard_map/ppermute | solution.py:355
  14.7 2.7 %shard_map.96 = (bf16[256,2176]{1,0:T(8,128)(2,1)}, bf16[256,2176]{1,0:T(8,128)(2,1)}) custom-call(s32[1]{0:T(128)} %bitcast.y_ref, s32[1]{0:T(128)S(6)} %copy.10.length_ref, bf16[256,4608]{1,0:T(8,128)(2,1)} %own_ref.3, bf16[256,1024]{1,0:T(8,128)(2,1)} %cot_ref.5), custom_call_target="tpu_custom_call" | custom-call | tf_op jit(solution)/shard_map/pallas_call | solution.py:71
  19.9 18.4 %collective-permute-done.both_ref = bf16[256,2176]{1,0:T(8,128)(2,1)} collective-permute-done((bf16[256,2176]{1,0:T(8,128)(2,1)}, bf16[256,2176]{1,0:T(8,128)(2,1)}, u32[]{:S(2)}, u32[]{:S(2)}) %collective-permute-start) | collective-permute-done | bytes 1114144 | tf_op jit(solution)/shard_map/ppermute | solution.py:355
  38.3 13.9 %all-gather.2.cloned.1.call-done.weight_ref.after_ref = bf16[1152,1024]{1,0:T(8,128)(2,1)} async-done(((bf16[144,1024]{1,0:T(8,128)(2,1)}), bf16[1152,1024]{1,0:T(8,128)(2,1)}) %all-gather.2.cloned.1.call-update) | async-done | bytes 2359312 | tf_op jit(solution)/shard_map/all_gather | solution.py:381
  52.3 1.7 %copy-done.1 = bf16[1152,1024]{1,0:T(8,128)(2,1)S(1)} copy-done((bf16[1152,1024]{1,0:T(8,128)(2,1)S(1)}, bf16[1152,1024]{1,0:T(8,128)(2,1)}, u32[]{:S(2)}) %copy-start.1) | copy-done | bytes 2359320
  53.9 2.9 %shard_map.95 = (f32[256,1024]{1,0:T(8,128)S(1)}, bf16[256,1024]{1,0:T(8,128)(2,1)S(1)}) custom-call(s32[1]{0:T(128)} %bitcast.y_ref, bf16[256,4608]{1,0:T(8,128)(2,1)S(1)} %copy-done, bf16[256,2176]{1,0:T(8,128)(2,1)} %collective-permute-done.both_ref, bf16[1152,1024]{1,0:T(8,128)(2,1)S(1)} %copy-done.1), custom_call_target="tpu_custom_call" | custom-call | tf_op jit(solution)/shard_map/pallas_call | solution.py:185
  56.8 2.7 %shard_map.100.first_ref = f32[1152,1024]{1,0:T(8,128)S(1)} custom-call(s32[1]{0:T(128)} %bitcast.y_ref, s32[1]{0:T(128)S(6)} %copy.10.length_ref, bf16[256,4608]{1,0:T(8,128)(2,1)S(1)} %copy-done, bf16[256,1024]{1,0:T(8,128)(2,1)S(1)} %copy-done.3, bf16[256,2176]{1,0:T(8,128)(2,1)} %collective-permute-done.both_ref, bf16[1152,1024]{1,0:T(8,128)(2,1)S(1)} %copy-done.1), custom_call_target="tpu_custom_call" | custom-call | tf_op jit(solution)/shard_map/pallas_call | solution.py:106
  59.5 3.8 %collective-permute-done.2.one_ref = bf16[256,2176]{1,0:T(8,128)(2,1)} collective-permute-done((bf16[256,2176]{1,0:T(8,128)(2,1)}, bf16[256,2176]{1,0:T(8,128)(2,1)}, u32[]{:S(2)}, u32[]{:S(2)}) %collective-permute-start.2) | collective-permute-done | bytes 1114144 | tf_op jit(solution)/shard_map/ppermute | solution.py:355
  63.9 3.4 %shard_map.101 = (f32[4,144,512]{2,1,0:T(8,128)S(1)}, bf16[4,144,512]{2,1,0:T(8,128)(2,1)S(1)}, f32[4,144,512]{2,1,0:T(8,128)S(1)}, bf16[4,144,512]{2,1,0:T(8,128)(2,1)S(1)}) custom-call(s32[2]{0:T(128)S(1)} %pad_add_fusion.place_ref, f32[1152,1024]{1,0:T(8,128)S(1)} %shard_map.100.first_ref, bf16[256,2176]{1,0:T(8,128)(2,1)} %collective-permute-done.2.one_ref, ...), custom_call_target="tpu_custom_call" | custom-call | tf_op jit(solution)/shard_map/pallas_call | solution.py:149
  67.3 5.7 %collective-permute-start.6 = (bf16[4,144,512]{2,1,0:T(8,128)(2,1)S(1)}, bf16[4,144,512]{2,1,0:T(8,128)(2,1)S(1)}, u32[]{:S(2)}, u32[]{:S(2)}) collective-permute-start(bf16[4,144,512]{2,1,0:T(8,128)(2,1)S(1)} %get-tuple-element.35), channel_id=1, source_target_pairs={{0,1},{1,0},{2,3},{3,2},{4,5},{5,4},{6,7},{7,6},{32,39},{33,34},{3... | collective-permute-start | bytes 1769480 | tf_op jit(solution)/shard_map/ppermute | solution.py:364
  73.1 2.9 %collective-permute-start.1 = (bf16[256,1024]{1,0:T(8,128)(2,1)S(1)}, bf16[256,1024]{1,0:T(8,128)(2,1)S(1)}, u32[]{:S(2)}, u32[]{:S(2)}) collective-permute-start(bf16[256,1024]{1,0:T(8,128)(2,1)S(1)} %get-tuple-element.28.refs_0_), channel_id=1, source_target_pairs={{0,16},{8,24},{16,0},{24,8},{1,17},{9,25},{17,1},{25,9},{2,18},{10... | collective-permute-start | bytes 1572872 | tf_op jit(solution)/shard_map/ppermute | solution.py:355
  76.1 3.1 %shard_map.97 = (bf16[256,1024]{1,0:T(8,128)(2,1)S(1)}, bf16[256,1024]{1,0:T(8,128)(2,1)S(1)}) custom-call(bf16[256,2176]{1,0:T(8,128)(2,1)} %collective-permute-done.2.one_ref, bf16[256,2176]{1,0:T(8,128)(2,1)} %collective-permute-done.3.two_ref, bf16[1152,1024]{1,0:T(8,128)(2,1)S(1)} %copy-done.2), custom_call_target="tpu_custom_call" | custom-call | tf_op jit(solution)/shard_map/pallas_call | solution.py:206
  80.8 5.2 %collective-permute-done.1.one_ref.rest_0_ = bf16[256,1024]{1,0:T(8,128)(2,1)S(1)} collective-permute-done((bf16[256,1024]{1,0:T(8,128)(2,1)S(1)}, bf16[256,1024]{1,0:T(8,128)(2,1)S(1)}, u32[]{:S(2)}, u32[]{:S(2)}) %collective-permute-start.1) | collective-permute-done | bytes 524320 | tf_op jit(solution)/shard_map/ppermute | solution.py:355
  86.0 4.3 %collective-permute-done.9.got_ref = bf16[4,144,512]{2,1,0:T(8,128)(2,1)S(1)} collective-permute-done((bf16[4,144,512]{2,1,0:T(8,128)(2,1)S(1)}, bf16[4,144,512]{2,1,0:T(8,128)(2,1)S(1)}, u32[]{:S(2)}, u32[]{:S(2)}) %collective-permute-start.9) | collective-permute-done | bytes 589856 | tf_op jit(solution)/shard_map/ppermute | solution.py:364
  90.5 1.6 %collective-permute-start.4 = (bf16[256,1024]{1,0:T(8,128)(2,1)S(1)}, bf16[256,1024]{1,0:T(8,128)(2,1)S(1)}, u32[]{:S(2)}, u32[]{:S(2)}) collective-permute-start(bf16[256,1024]{1,0:T(8,128)(2,1)S(1)} %get-tuple-element.31.rest_0_), channel_id=1, source_target_pairs={{0,8},{8,0},{16,24},{24,16},{1,9},{9,1},{17,25},{25,17},{2,10},{10... | collective-permute-start | bytes 1572872 | tf_op jit(solution)/shard_map/ppermute | solution.py:355
  92.2 2.1 %collective-permute-start.5 = (bf16[256,1024]{1,0:T(8,128)(2,1)S(1)}, bf16[256,1024]{1,0:T(8,128)(2,1)S(1)}, u32[]{:S(2)}, u32[]{:S(2)}) collective-permute-start(bf16[256,1024]{1,0:T(8,128)(2,1)S(1)} %get-tuple-element.32.rest_1_), channel_id=1, source_target_pairs={{0,24},{8,16},{16,8},{24,0},{1,25},{9,17},{17,9},{25,1},{2,26},{10... | collective-permute-start | bytes 1572872 | tf_op jit(solution)/shard_map/ppermute | solution.py:355
  94.9 3.8 %collective-permute-start.8 = (bf16[144,512]{1,0:T(8,128)(2,1)S(1)}, bf16[144,512]{1,0:T(8,128)(2,1)S(1)}, u32[]{:S(2)}, u32[]{:S(2)}) collective-permute-start(bf16[144,512]{1,0:T(8,128)(2,1)S(1)} %fusion), channel_id=1, source_target_pairs={{0,7},{1,2},{2,1},{3,4},{4,3},{5,6},{6,5},{7,0},{32,33},{33,32},{3... | collective-permute-start | bytes 442376 | tf_op jit(solution)/shard_map/ppermute | solution.py:364
  98.7 2.9 %collective-permute-start.11 = (bf16[144,512]{1,0:T(8,128)(2,1)S(1)}, bf16[144,512]{1,0:T(8,128)(2,1)S(1)}, u32[]{:S(2)}, u32[]{:S(2)}) collective-permute-start(bf16[144,512]{1,0:T(8,128)(2,1)S(1)} %fusion.1), channel_id=1, source_target_pairs={{0,7},{1,2},{2,1},{3,4},{4,3},{5,6},{6,5},{7,0},{32,33},{33,32},{3... | collective-permute-start | bytes 442376 | tf_op jit(solution)/shard_map/ppermute | solution.py:364
  101.6 2.2 %collective-permute-done.8.last_ref = bf16[144,512]{1,0:T(8,128)(2,1)S(1)} collective-permute-done((bf16[144,512]{1,0:T(8,128)(2,1)S(1)}, bf16[144,512]{1,0:T(8,128)(2,1)S(1)}, u32[]{:S(2)}, u32[]{:S(2)}) %collective-permute-start.8) | collective-permute-done | bytes 147488 | tf_op jit(solution)/shard_map/ppermute | solution.py:364
  104.2 2.6 %collective-permute-start.14 = (bf16[144,256]{1,0:T(8,128)(2,1)S(1)}, bf16[144,256]{1,0:T(8,128)(2,1)S(1)}, u32[]{:S(2)}, u32[]{:S(2)}) collective-permute-start(bf16[144,256]{1,0:T(8,128)(2,1)S(1)} %get-tuple-element.47.refs_0_), channel_id=1, source_target_pairs={{0,192},{64,128},{128,64},{192,0},{1,193},{65,129},{129,65},{193,1... | collective-permute-start | bytes 221192 | tf_op jit(solution)/shard_map/ppermute | solution.py:355
  108.0 2.6 %collective-permute-start.17 = (bf16[144,256]{1,0:T(8,128)(2,1)S(1)}, bf16[144,256]{1,0:T(8,128)(2,1)S(1)}, u32[]{:S(2)}, u32[]{:S(2)}) collective-permute-start(bf16[144,256]{1,0:T(8,128)(2,1)S(1)} %get-tuple-element.48.refs_4_), channel_id=1, source_target_pairs={{0,192},{64,128},{128,64},{192,0},{1,193},{65,129},{129,65},{193,1... | collective-permute-start | bytes 221192 | tf_op jit(solution)/shard_map/ppermute | solution.py:355
  113.9 2.2 %collective-permute-done.16.refs_6_ = bf16[144,256]{1,0:T(8,128)(2,1)S(1)} collective-permute-done((bf16[144,256]{1,0:T(8,128)(2,1)S(1)}, bf16[144,256]{1,0:T(8,128)(2,1)S(1)}, u32[]{:S(2)}, u32[]{:S(2)}) %collective-permute-start.16) | collective-permute-done | bytes 73760 | tf_op jit(solution)/shard_map/ppermute | solution.py:355
  116.1 3.7 %collective-permute-start.18 = (f32[144,512]{1,0:T(8,128)S(1)}, f32[144,512]{1,0:T(8,128)S(1)}, u32[]{:S(2)}, u32[]{:S(2)}) collective-permute-start(f32[144,512]{1,0:T(8,128)S(1)} %shard_map.107.mine_ref), channel_id=1, source_target_pairs={{0,32},{32,0},{1,33},{33,1},{2,34},{34,2},{3,35},{35,3},{4,36},{36... | collective-permute-start | bytes 884744 | tf_op jit(solution)/shard_map/ppermute | solution.py:355
  (51 shorter events, 14.1 us)
Async XLA Ops:
  7.2 45.1 %all-gather.2.cloned.1.call-start = ((), (), s32[]{:S(2)}) async-start(), calls=%async_computation | async-start | bytes 2654208 | tf_op jit(solution)/shard_map/all_gather | solution.py:381
  10.8 41.4 %copy-start = (bf16[256,4608]{1,0:T(8,128)(2,1)S(1)}, bf16[256,4608]{1,0:T(8,128)(2,1)}, u32[]{:S(2)}) copy-start(bf16[256,4608]{1,0:T(8,128)(2,1)} %own_ref.3) | copy-start | bytes 7077892
  10.8 27.5 %collective-permute-start = (bf16[256,2176]{1,0:T(8,128)(2,1)}, bf16[256,2176]{1,0:T(8,128)(2,1)}, u32[]{:S(2)}, u32[]{:S(2)}) collective-permute-start(bf16[256,2176]{1,0:T(8,128)(2,1)} %shard_map.94), channel_id=1, source_target_pairs={{0,16},{8,24},{16,0},{24,8},{1,17},{9,25},{17,1},{25,9},{2,18},{10... | collective-permute-start | bytes 3342344 | tf_op jit(solution)/shard_map/ppermute | solution.py:355
  17.4 45.9 %collective-permute-start.2 = (bf16[256,2176]{1,0:T(8,128)(2,1)}, bf16[256,2176]{1,0:T(8,128)(2,1)}, u32[]{:S(2)}, u32[]{:S(2)}) collective-permute-start(bf16[256,2176]{1,0:T(8,128)(2,1)} %get-tuple-element.29), channel_id=1, source_target_pairs={{0,8},{8,0},{16,24},{24,16},{1,9},{9,1},{17,25},{25,17},{2,10},{10... | collective-permute-start | bytes 3342344 | tf_op jit(solution)/shard_map/ppermute | solution.py:355
  17.9 46.0 %collective-permute-start.3 = (bf16[256,2176]{1,0:T(8,128)(2,1)}, bf16[256,2176]{1,0:T(8,128)(2,1)}, u32[]{:S(2)}, u32[]{:S(2)}) collective-permute-start(bf16[256,2176]{1,0:T(8,128)(2,1)} %get-tuple-element.30), channel_id=1, source_target_pairs={{0,24},{8,16},{16,8},{24,0},{1,25},{9,17},{17,9},{25,1},{2,26},{10... | collective-permute-start | bytes 3342344 | tf_op jit(solution)/shard_map/ppermute | solution.py:355
  63.9 12.2 %copy-start.2 = (bf16[1152,1024]{1,0:T(8,128)(2,1)S(1)}, bf16[1152,1024]{1,0:T(8,128)(2,1)}, u32[]{:S(2)}) copy-start(bf16[1152,1024]{1,0:T(8,128)(2,1)} %all-gather.2.cloned.1.call-done.weight_ref.after_ref) | copy-start | bytes 7077892
  67.3 13.3 %collective-permute-start.6 = (bf16[4,144,512]{2,1,0:T(8,128)(2,1)S(1)}, bf16[4,144,512]{2,1,0:T(8,128)(2,1)S(1)}, u32[]{:S(2)}, u32[]{:S(2)}) collective-permute-start(bf16[4,144,512]{2,1,0:T(8,128)(2,1)S(1)} %get-tuple-element.35), channel_id=1, source_target_pairs={{0,1},{1,0},{2,3},{3,2},{4,5},{5,4},{6,7},{7,6},{32,39},{33,34},{3... | collective-permute-start | bytes 1769480 | tf_op jit(solution)/shard_map/ppermute | solution.py:364
  73.0 17.2 %collective-permute-start.9 = (bf16[4,144,512]{2,1,0:T(8,128)(2,1)S(1)}, bf16[4,144,512]{2,1,0:T(8,128)(2,1)S(1)}, u32[]{:S(2)}, u32[]{:S(2)}) collective-permute-start(bf16[4,144,512]{2,1,0:T(8,128)(2,1)S(1)} %get-tuple-element.41), channel_id=1, source_target_pairs={{0,1},{1,0},{2,3},{3,2},{4,5},{5,4},{6,7},{7,6},{32,39},{33,34},{3... | collective-permute-start | bytes 1769480 | tf_op jit(solution)/shard_map/ppermute | solution.py:364
  73.1 12.8 %collective-permute-start.1 = (bf16[256,1024]{1,0:T(8,128)(2,1)S(1)}, bf16[256,1024]{1,0:T(8,128)(2,1)S(1)}, u32[]{:S(2)}, u32[]{:S(2)}) collective-permute-start(bf16[256,1024]{1,0:T(8,128)(2,1)S(1)} %get-tuple-element.28.refs_0_), channel_id=1, source_target_pairs={{0,16},{8,24},{16,0},{24,8},{1,17},{9,25},{17,1},{25,9},{2,18},{10... | collective-permute-start | bytes 1572872 | tf_op jit(solution)/shard_map/ppermute | solution.py:355
  80.7 14.1 %collective-permute-start.7 = (bf16[2,144,512]{2,1,0:T(8,128)(2,1)S(1)}, bf16[2,144,512]{2,1,0:T(8,128)(2,1)S(1)}, u32[]{:S(2)}, u32[]{:S(2)}) collective-permute-start(bf16[2,144,512]{2,1,0:T(8,128)(2,1)S(1)} %get-tuple-element.37), channel_id=1, source_target_pairs={{0,6},{1,3},{2,0},{3,5},{4,2},{5,7},{6,4},{7,1},{32,34},{33,39},{3... | collective-permute-start | bytes 884744 | tf_op jit(solution)/shard_map/ppermute | solution.py:364
  90.4 13.4 %copy-start.4 = (f32[1,144,1024]{2,1,0:T(8,128)S(1)}, f32[1,144,1024]{2,1,0:T(8,128)}, u32[]{:S(2)}) copy-start(f32[1,144,1024]{2,1,0:T(8,128)} %param.10) | copy-start | bytes 1769476
  90.4 13.4 %copy-start.5 = (f32[256,128]{1,0:T(8,128)S(1)}, f32[256,128]{1,0:T(8,128)}, u32[]{:S(2)}) copy-start(f32[256,128]{1,0:T(8,128)} %constant.32.clone.table_ref) | copy-start | bytes 393220
  90.4 8.3 %collective-permute-start.10 = (bf16[2,144,512]{2,1,0:T(8,128)(2,1)S(1)}, bf16[2,144,512]{2,1,0:T(8,128)(2,1)S(1)}, u32[]{:S(2)}, u32[]{:S(2)}) collective-permute-start(bf16[2,144,512]{2,1,0:T(8,128)(2,1)S(1)} %get-tuple-element.43), channel_id=1, source_target_pairs={{0,6},{1,3},{2,0},{3,5},{4,2},{5,7},{6,4},{7,1},{32,34},{33,39},{3... | collective-permute-start | bytes 884744 | tf_op jit(solution)/shard_map/ppermute | solution.py:364
  90.5 16.8 %collective-permute-start.4 = (bf16[256,1024]{1,0:T(8,128)(2,1)S(1)}, bf16[256,1024]{1,0:T(8,128)(2,1)S(1)}, u32[]{:S(2)}, u32[]{:S(2)}) collective-permute-start(bf16[256,1024]{1,0:T(8,128)(2,1)S(1)} %get-tuple-element.31.rest_0_), channel_id=1, source_target_pairs={{0,8},{8,0},{16,24},{24,16},{1,9},{9,1},{17,25},{25,17},{2,10},{10... | collective-permute-start | bytes 1572872 | tf_op jit(solution)/shard_map/ppermute | solution.py:355
  92.2 15.4 %collective-permute-start.5 = (bf16[256,1024]{1,0:T(8,128)(2,1)S(1)}, bf16[256,1024]{1,0:T(8,128)(2,1)S(1)}, u32[]{:S(2)}, u32[]{:S(2)}) collective-permute-start(bf16[256,1024]{1,0:T(8,128)(2,1)S(1)} %get-tuple-element.32.rest_1_), channel_id=1, source_target_pairs={{0,24},{8,16},{16,8},{24,0},{1,25},{9,17},{17,9},{25,1},{2,26},{10... | collective-permute-start | bytes 1572872 | tf_op jit(solution)/shard_map/ppermute | solution.py:355
  94.9 8.9 %collective-permute-start.8 = (bf16[144,512]{1,0:T(8,128)(2,1)S(1)}, bf16[144,512]{1,0:T(8,128)(2,1)S(1)}, u32[]{:S(2)}, u32[]{:S(2)}) collective-permute-start(bf16[144,512]{1,0:T(8,128)(2,1)S(1)} %fusion), channel_id=1, source_target_pairs={{0,7},{1,2},{2,1},{3,4},{4,3},{5,6},{6,5},{7,0},{32,33},{33,32},{3... | collective-permute-start | bytes 442376 | tf_op jit(solution)/shard_map/ppermute | solution.py:364
  98.7 8.9 %collective-permute-start.11 = (bf16[144,512]{1,0:T(8,128)(2,1)S(1)}, bf16[144,512]{1,0:T(8,128)(2,1)S(1)}, u32[]{:S(2)}, u32[]{:S(2)}) collective-permute-start(bf16[144,512]{1,0:T(8,128)(2,1)S(1)} %fusion.1), channel_id=1, source_target_pairs={{0,7},{1,2},{2,1},{3,4},{4,3},{5,6},{6,5},{7,0},{32,33},{33,32},{3... | collective-permute-start | bytes 442376 | tf_op jit(solution)/shard_map/ppermute | solution.py:364
  104.2 6.9 %collective-permute-start.14 = (bf16[144,256]{1,0:T(8,128)(2,1)S(1)}, bf16[144,256]{1,0:T(8,128)(2,1)S(1)}, u32[]{:S(2)}, u32[]{:S(2)}) collective-permute-start(bf16[144,256]{1,0:T(8,128)(2,1)S(1)} %get-tuple-element.47.refs_0_), channel_id=1, source_target_pairs={{0,192},{64,128},{128,64},{192,0},{1,193},{65,129},{129,65},{193,1... | collective-permute-start | bytes 221192 | tf_op jit(solution)/shard_map/ppermute | solution.py:355
  106.8 7.1 %collective-permute-start.13 = (bf16[144,256]{1,0:T(8,128)(2,1)S(1)}, bf16[144,256]{1,0:T(8,128)(2,1)S(1)}, u32[]{:S(2)}, u32[]{:S(2)}) collective-permute-start(bf16[144,256]{1,0:T(8,128)(2,1)S(1)} %get-tuple-element.47.refs_0_), channel_id=1, source_target_pairs={{0,128},{64,192},{128,0},{192,64},{1,129},{65,193},{129,1},{193,65... | collective-permute-start | bytes 221192 | tf_op jit(solution)/shard_map/ppermute | solution.py:355
  107.3 6.6 %collective-permute-start.12 = (bf16[144,256]{1,0:T(8,128)(2,1)S(1)}, bf16[144,256]{1,0:T(8,128)(2,1)S(1)}, u32[]{:S(2)}, u32[]{:S(2)}) collective-permute-start(bf16[144,256]{1,0:T(8,128)(2,1)S(1)} %get-tuple-element.47.refs_0_), channel_id=1, source_target_pairs={{0,64},{64,0},{128,192},{192,128},{1,65},{65,1},{129,193},{193,129... | collective-permute-start | bytes 221192 | tf_op jit(solution)/shard_map/ppermute | solution.py:355
  108.0 5.8 %collective-permute-start.17 = (bf16[144,256]{1,0:T(8,128)(2,1)S(1)}, bf16[144,256]{1,0:T(8,128)(2,1)S(1)}, u32[]{:S(2)}, u32[]{:S(2)}) collective-permute-start(bf16[144,256]{1,0:T(8,128)(2,1)S(1)} %get-tuple-element.48.refs_4_), channel_id=1, source_target_pairs={{0,192},{64,128},{128,64},{192,0},{1,193},{65,129},{129,65},{193,1... | collective-permute-start | bytes 221192 | tf_op jit(solution)/shard_map/ppermute | solution.py:355
  110.6 5.4 %collective-permute-start.16 = (bf16[144,256]{1,0:T(8,128)(2,1)S(1)}, bf16[144,256]{1,0:T(8,128)(2,1)S(1)}, u32[]{:S(2)}, u32[]{:S(2)}) collective-permute-start(bf16[144,256]{1,0:T(8,128)(2,1)S(1)} %get-tuple-element.48.refs_4_), channel_id=1, source_target_pairs={{0,128},{64,192},{128,0},{192,64},{1,129},{65,193},{129,1},{193,65... | collective-permute-start | bytes 221192 | tf_op jit(solution)/shard_map/ppermute | solution.py:355
  111.1 4.9 %collective-permute-start.15 = (bf16[144,256]{1,0:T(8,128)(2,1)S(1)}, bf16[144,256]{1,0:T(8,128)(2,1)S(1)}, u32[]{:S(2)}, u32[]{:S(2)}) collective-permute-start(bf16[144,256]{1,0:T(8,128)(2,1)S(1)} %get-tuple-element.48.refs_4_), channel_id=1, source_target_pairs={{0,64},{64,0},{128,192},{192,128},{1,65},{65,1},{129,193},{193,129... | collective-permute-start | bytes 221192 | tf_op jit(solution)/shard_map/ppermute | solution.py:355
  116.1 4.9 %collective-permute-start.18 = (f32[144,512]{1,0:T(8,128)S(1)}, f32[144,512]{1,0:T(8,128)S(1)}, u32[]{:S(2)}, u32[]{:S(2)}) collective-permute-start(f32[144,512]{1,0:T(8,128)S(1)} %shard_map.107.mine_ref), channel_id=1, source_target_pairs={{0,32},{32,0},{1,33},{33,1},{2,34},{34,2},{3,35},{35,3},{4,36},{36... | collective-permute-start | bytes 884744 | tf_op jit(solution)/shard_map/ppermute | solution.py:355
  (4 other events, 13.1 us)
Sparse Core Ops, SparseCore 0:
  9.8 42.4 all-gather.1

commit v2 on v1

--- a/solution.py
+++ b/solution.py
@@ -332,7 +332,8 @@
     )(*parts, *after)
 
 
-def decode_kernel(mine_ref, other_ref, table_t_ref, update_ref):
+def decode_kernel(mine_ref, other_ref, table_t_ref, *rest):
+    update_ref = rest[-1]
     for g in range(update_ref.shape[1] // GROUP):
         lanes = slice(g * 128, (g + 1) * 128)
         coeffs = mine_ref[:, lanes] + other_ref[:, lanes]
@@ -341,14 +342,20 @@
         )
 
 
-def decode(mine, other, table, width):
+def decode(h, mine, other, table, width, made):
+    rows, lanes = mine.shape
+    cols = lanes // 128 * GROUP
+    whole_block = lambda array: pl.BlockSpec(array.shape, lambda i: (0, 0))
+    operands = (mine, other, table.T)
     return pl.pallas_call(
         decode_kernel,
-        out_shape=jax.ShapeDtypeStruct((mine.shape[0], width), F32),
-        in_specs=[VMEM] * 3,
-        out_specs=VMEM,
-        compiler_params=PARAMS,
-    )(mine, other, table.T)
+        grid=(1,),
+        out_shape=jax.ShapeDtypeStruct((rows, width), F32),
+        in_specs=[whole_block(array) for array in operands] + [pl.BlockSpec(memory_space=pl.ANY)] * len(made),
+        out_specs=pl.BlockSpec((rows, cols), lambda i: (0, h)),
+        input_output_aliases={len(operands): 0} if made else {},
+        compiler_params=PARAMS,
+    )(*operands, *made)
 
 
 def swap(array, axis, d):
@@ -403,8 +410,12 @@
 
     projected, projected_token = finish_projection(total, backs)
     new_momentum, new_token = subtract_rebuilt(table, blends, momentum.shape[1:])
-    mine = combine(sums, (projected_token, new_token))
-    update = decode(mine, swap(mine, "core", 1), table, width)
+    made = ()
+    for h in range(HALVES):
+        after = (projected_token, new_token) if h == HALVES - 1 else ()
+        mine = combine(sums[4 * h : 4 * h + 4], after)
+        made = (decode(h, mine, swap(mine, "core", 1), table, width, made),)
+    (update,) = made
     return (projected, new_momentum[None], update)
 
 

time: 130 us -> 129 us (level)
  waiting for transfers between devices: 54.5 us -> 51.2 us
  starting transfers between devices: 34.5 us -> 36.5 us
    ppermute x13 -> x14, waiting for transfers between devices: 31.4 us -> 28 us  [swap(): lax.ppermute(array, axis, [(i, i ^ d) for i in range(lax.axis_size(axis))])]
    ppermute x13 -> x14, starting transfers between devices: 21.8 us -> 24 us  [swap(): lax.ppermute(array, axis, [(i, i ^ d) for i in range(lax.axis_size(axis))])]
  transfers between devices with their start and end apart: 20 -> 21, of which waited for: 11 -> 10; matrix products, arithmetic and copies ran while one was open for 0% -> 0% of each run, Pallas kernels for 14% -> 15%
where the time goes in v2:
time: 129 us
  waiting for transfers between devices  51.2 us (40%)
  starting transfers between devices  36.5 us (28%)
  Pallas kernels  24.5 us (19%)
  between operations  14.8 us (11%)
  local copies, waits for them, and re-layouts  1.7 us (1%)
    ppermute x14, waiting for transfers between devices, swap(): lax.ppermute(array, axis, [(i, i ^ d) for i in range(lax.axis_size(axis))])  28 us
    ppermute x14, starting transfers between devices, swap(): lax.ppermute(array, axis, [(i, i ^ d) for i in range(lax.axis_size(axis))])  24 us
    all_gather x1, waiting for transfers between devices, per_device(): weight_quarter = lax.all_gather(weight, 'z', axis=0, tiled=True)  13.9 us
    ppermute x6, starting transfers between devices, move(): lax.ppermute(array, ('core', 'z'), [(c * nz + z, c * nz + (z + steps * si...  12.4 us
    ppermute x6, waiting for transfers between devices, move(): lax.ppermute(array, ('core', 'z'), [(c * nz + z, c * nz + (z + steps * si...  8.59 us
    pallas_call x2, Pallas kernels, split_inputs(): pl.pallas_call(functools.partial(split_kernel, order), out_shape=[jax.Sha...  4.97 us
    pallas_call x1, Pallas kernels, grad_terms(): pl.pallas_call(functools.partial(grad_kernel, nz, len(after)), out_shape=...  3.44 us
    pallas_call x1, Pallas kernels, project_rest(): pl.pallas_call(project_kernel, out_shape=[shape, shape], in_specs=[VMEM]...  3.14 us
  transfers between devices with their start and end apart: 21, of which 10 were waited for; matrix products, arithmetic and copies ran while one was open for 0% of the time, Pallas kernels for 15%

profile of v2, /device:TPU:1, one launch (start us, length us, event | category | flops | bytes accessed | tf_op | source)
XLA Modules:
  0.0 128.8 jit_solution(7066246532547619090)
XLA Ops:
  8.5 2.3 %shard_map.94 = bf16[256,2176]{1,0:T(8,128)(2,1)} custom-call(s32[1]{0:T(128)} %bitcast.y_ref, s32[1]{0:T(128)S(6)} %copy.12.length_ref, bf16[256,4608]{1,0:T(8,128)(2,1)} %own_ref.3, bf16[256,1024]{1,0:T(8,128)(2,1)} %cot_ref.5), custom_call_target="tpu_custom_call" | custom-call | tf_op jit(solution)/shard_map/pallas_call | solution.py:71
  10.9 3.8 %collective-permute-start = (bf16[256,2176]{1,0:T(8,128)(2,1)}, bf16[256,2176]{1,0:T(8,128)(2,1)}, u32[]{:S(2)}, u32[]{:S(2)}) collective-permute-start(bf16[256,2176]{1,0:T(8,128)(2,1)} %shard_map.94), channel_id=1, source_target_pairs={{0,16},{8,24},{16,0},{24,8},{1,17},{9,25},{17,1},{25,9},{2,18},{10... | collective-permute-start | bytes 3342344 | tf_op jit(solution)/shard_map/ppermute | solution.py:362
  14.7 2.7 %shard_map.96 = (bf16[256,2176]{1,0:T(8,128)(2,1)}, bf16[256,2176]{1,0:T(8,128)(2,1)}) custom-call(s32[1]{0:T(128)} %bitcast.y_ref, s32[1]{0:T(128)S(6)} %copy.12.length_ref, bf16[256,4608]{1,0:T(8,128)(2,1)} %own_ref.3, bf16[256,1024]{1,0:T(8,128)(2,1)} %cot_ref.5), custom_call_target="tpu_custom_call" | custom-call | tf_op jit(solution)/shard_map/pallas_call | solution.py:71
  19.9 18.4 %collective-permute-done.both_ref = bf16[256,2176]{1,0:T(8,128)(2,1)} collective-permute-done((bf16[256,2176]{1,0:T(8,128)(2,1)}, bf16[256,2176]{1,0:T(8,128)(2,1)}, u32[]{:S(2)}, u32[]{:S(2)}) %collective-permute-start) | collective-permute-done | bytes 1114144 | tf_op jit(solution)/shard_map/ppermute | solution.py:362
  38.3 13.9 %all-gather.2.cloned.1.call-done.weight_ref.after_ref = bf16[1152,1024]{1,0:T(8,128)(2,1)} async-done(((bf16[144,1024]{1,0:T(8,128)(2,1)}), bf16[1152,1024]{1,0:T(8,128)(2,1)}) %all-gather.2.cloned.1.call-update) | async-done | bytes 2359312 | tf_op jit(solution)/shard_map/all_gather | solution.py:388
  52.3 1.7 %copy-done.1 = bf16[1152,1024]{1,0:T(8,128)(2,1)S(1)} copy-done((bf16[1152,1024]{1,0:T(8,128)(2,1)S(1)}, bf16[1152,1024]{1,0:T(8,128)(2,1)}, u32[]{:S(2)}) %copy-start.1) | copy-done | bytes 2359320
  53.9 2.9 %shard_map.95 = (f32[256,1024]{1,0:T(8,128)S(1)}, bf16[256,1024]{1,0:T(8,128)(2,1)S(1)}) custom-call(s32[1]{0:T(128)} %bitcast.y_ref, bf16[256,4608]{1,0:T(8,128)(2,1)S(1)} %copy-done, bf16[256,2176]{1,0:T(8,128)(2,1)} %collective-permute-done.both_ref, bf16[1152,1024]{1,0:T(8,128)(2,1)S(1)} %copy-done.1), custom_call_target="tpu_custom_call" | custom-call | tf_op jit(solution)/shard_map/pallas_call | solution.py:185
  56.8 2.7 %shard_map.100.first_ref = f32[1152,1024]{1,0:T(8,128)S(1)} custom-call(s32[1]{0:T(128)} %bitcast.y_ref, s32[1]{0:T(128)S(6)} %copy.12.length_ref, bf16[256,4608]{1,0:T(8,128)(2,1)S(1)} %copy-done, bf16[256,1024]{1,0:T(8,128)(2,1)S(1)} %copy-done.3, bf16[256,2176]{1,0:T(8,128)(2,1)} %collective-permute-done.both_ref, bf16[1152,1024]{1,0:T(8,128)(2,1)S(1)} %copy-done.1), custom_call_target="tpu_custom_call" | custom-call | tf_op jit(solution)/shard_map/pallas_call | solution.py:106
  59.5 3.8 %collective-permute-done.2.one_ref = bf16[256,2176]{1,0:T(8,128)(2,1)} collective-permute-done((bf16[256,2176]{1,0:T(8,128)(2,1)}, bf16[256,2176]{1,0:T(8,128)(2,1)}, u32[]{:S(2)}, u32[]{:S(2)}) %collective-permute-start.2) | collective-permute-done | bytes 1114144 | tf_op jit(solution)/shard_map/ppermute | solution.py:362
  63.9 3.4 %shard_map.101 = (f32[4,144,512]{2,1,0:T(8,128)S(1)}, bf16[4,144,512]{2,1,0:T(8,128)(2,1)S(1)}, f32[4,144,512]{2,1,0:T(8,128)S(1)}, bf16[4,144,512]{2,1,0:T(8,128)(2,1)S(1)}) custom-call(s32[2]{0:T(128)S(1)} %pad_add_fusion.place_ref, f32[1152,1024]{1,0:T(8,128)S(1)} %shard_map.100.first_ref, bf16[256,2176]{1,0:T(8,128)(2,1)} %collective-permute-done.2.one_ref, ...), custom_call_target="tpu_custom_call" | custom-call | tf_op jit(solution)/shard_map/pallas_call | solution.py:149
  67.4 5.7 %collective-permute-start.6 = (bf16[4,144,512]{2,1,0:T(8,128)(2,1)S(1)}, bf16[4,144,512]{2,1,0:T(8,128)(2,1)S(1)}, u32[]{:S(2)}, u32[]{:S(2)}) collective-permute-start(bf16[4,144,512]{2,1,0:T(8,128)(2,1)S(1)} %get-tuple-element.35), channel_id=1, source_target_pairs={{0,1},{1,0},{2,3},{3,2},{4,5},{5,4},{6,7},{7,6},{32,39},{33,34},{3... | collective-permute-start | bytes 1769480 | tf_op jit(solution)/shard_map/ppermute | solution.py:371
  73.2 2.9 %collective-permute-start.1 = (bf16[256,1024]{1,0:T(8,128)(2,1)S(1)}, bf16[256,1024]{1,0:T(8,128)(2,1)S(1)}, u32[]{:S(2)}, u32[]{:S(2)}) collective-permute-start(bf16[256,1024]{1,0:T(8,128)(2,1)S(1)} %get-tuple-element.28.refs_0_), channel_id=1, source_target_pairs={{0,16},{8,24},{16,0},{24,8},{1,17},{9,25},{17,1},{25,9},{2,18},{10... | collective-permute-start | bytes 1572872 | tf_op jit(solution)/shard_map/ppermute | solution.py:362
  76.1 3.1 %shard_map.97 = (bf16[256,1024]{1,0:T(8,128)(2,1)S(1)}, bf16[256,1024]{1,0:T(8,128)(2,1)S(1)}) custom-call(bf16[256,2176]{1,0:T(8,128)(2,1)} %collective-permute-done.2.one_ref, bf16[256,2176]{1,0:T(8,128)(2,1)} %collective-permute-done.3.two_ref, bf16[1152,1024]{1,0:T(8,128)(2,1)S(1)} %copy-done.2), custom_call_target="tpu_custom_call" | custom-call | tf_op jit(solution)/shard_map/pallas_call | solution.py:206
  80.9 5.2 %collective-permute-done.1.one_ref.rest_0_ = bf16[256,1024]{1,0:T(8,128)(2,1)S(1)} collective-permute-done((bf16[256,1024]{1,0:T(8,128)(2,1)S(1)}, bf16[256,1024]{1,0:T(8,128)(2,1)S(1)}, u32[]{:S(2)}, u32[]{:S(2)}) %collective-permute-start.1) | collective-permute-done | bytes 524320 | tf_op jit(solution)/shard_map/ppermute | solution.py:362
  86.0 4.2 %collective-permute-done.9.got_ref = bf16[4,144,512]{2,1,0:T(8,128)(2,1)S(1)} collective-permute-done((bf16[4,144,512]{2,1,0:T(8,128)(2,1)S(1)}, bf16[4,144,512]{2,1,0:T(8,128)(2,1)S(1)}, u32[]{:S(2)}, u32[]{:S(2)}) %collective-permute-start.9) | collective-permute-done | bytes 589856 | tf_op jit(solution)/shard_map/ppermute | solution.py:371
  90.4 1.7 %collective-permute-start.4 = (bf16[256,1024]{1,0:T(8,128)(2,1)S(1)}, bf16[256,1024]{1,0:T(8,128)(2,1)S(1)}, u32[]{:S(2)}, u32[]{:S(2)}) collective-permute-start(bf16[256,1024]{1,0:T(8,128)(2,1)S(1)} %get-tuple-element.31.rest_0_), channel_id=1, source_target_pairs={{0,8},{8,0},{16,24},{24,16},{1,9},{9,1},{17,25},{25,17},{2,10},{10... | collective-permute-start | bytes 1572872 | tf_op jit(solution)/shard_map/ppermute | solution.py:362
  92.1 2.1 %collective-permute-start.5 = (bf16[256,1024]{1,0:T(8,128)(2,1)S(1)}, bf16[256,1024]{1,0:T(8,128)(2,1)S(1)}, u32[]{:S(2)}, u32[]{:S(2)}) collective-permute-start(bf16[256,1024]{1,0:T(8,128)(2,1)S(1)} %get-tuple-element.32.rest_1_), channel_id=1, source_target_pairs={{0,24},{8,16},{16,8},{24,0},{1,25},{9,17},{17,9},{25,1},{2,26},{10... | collective-permute-start | bytes 1572872 | tf_op jit(solution)/shard_map/ppermute | solution.py:362
  95.0 3.7 %collective-permute-start.8 = (bf16[144,512]{1,0:T(8,128)(2,1)S(1)}, bf16[144,512]{1,0:T(8,128)(2,1)S(1)}, u32[]{:S(2)}, u32[]{:S(2)}) collective-permute-start(bf16[144,512]{1,0:T(8,128)(2,1)S(1)} %fusion), channel_id=1, source_target_pairs={{0,7},{1,2},{2,1},{3,4},{4,3},{5,6},{6,5},{7,0},{32,33},{33,32},{3... | collective-permute-start | bytes 442376 | tf_op jit(solution)/shard_map/ppermute | solution.py:371
  98.7 2.7 %collective-permute-start.11 = (bf16[144,512]{1,0:T(8,128)(2,1)S(1)}, bf16[144,512]{1,0:T(8,128)(2,1)S(1)}, u32[]{:S(2)}, u32[]{:S(2)}) collective-permute-start(bf16[144,512]{1,0:T(8,128)(2,1)S(1)} %fusion.1), channel_id=1, source_target_pairs={{0,7},{1,2},{2,1},{3,4},{4,3},{5,6},{6,5},{7,0},{32,33},{33,32},{3... | collective-permute-start | bytes 442376 | tf_op jit(solution)/shard_map/ppermute | solution.py:371
  101.5 2.2 %collective-permute-done.8.last_ref = bf16[144,512]{1,0:T(8,128)(2,1)S(1)} collective-permute-done((bf16[144,512]{1,0:T(8,128)(2,1)S(1)}, bf16[144,512]{1,0:T(8,128)(2,1)S(1)}, u32[]{:S(2)}, u32[]{:S(2)}) %collective-permute-start.8) | collective-permute-done | bytes 147488 | tf_op jit(solution)/shard_map/ppermute | solution.py:371
  104.1 2.6 %collective-permute-start.18 = (bf16[144,256]{1,0:T(8,128)(2,1)S(1)}, bf16[144,256]{1,0:T(8,128)(2,1)S(1)}, u32[]{:S(2)}, u32[]{:S(2)}) collective-permute-start(bf16[144,256]{1,0:T(8,128)(2,1)S(1)} %get-tuple-element.50.refs_0_), channel_id=1, source_target_pairs={{0,192},{64,128},{128,64},{192,0},{1,193},{65,129},{129,65},{193,1... | collective-permute-start | bytes 221192 | tf_op jit(solution)/shard_map/ppermute | solution.py:362
  108.0 2.6 %collective-permute-start.14 = (bf16[144,256]{1,0:T(8,128)(2,1)S(1)}, bf16[144,256]{1,0:T(8,128)(2,1)S(1)}, u32[]{:S(2)}, u32[]{:S(2)}) collective-permute-start(bf16[144,256]{1,0:T(8,128)(2,1)S(1)} %get-tuple-element.47.refs_0_), channel_id=1, source_target_pairs={{0,192},{64,128},{128,64},{192,0},{1,193},{65,129},{129,65},{193,1... | collective-permute-start | bytes 221192 | tf_op jit(solution)/shard_map/ppermute | solution.py:362
  113.8 3.9 %collective-permute-start.19 = (f32[144,256]{1,0:T(8,128)S(1)}, f32[144,256]{1,0:T(8,128)S(1)}, u32[]{:S(2)}, u32[]{:S(2)}) collective-permute-start(f32[144,256]{1,0:T(8,128)S(1)} %shard_map.108.mine_ref), channel_id=1, source_target_pairs={{0,32},{32,0},{1,33},{33,1},{2,34},{34,2},{3,35},{35,3},{4,36},{36... | collective-permute-start | bytes 442376 | tf_op jit(solution)/shard_map/ppermute | solution.py:362
  117.8 2.0 %collective-permute-start.15 = (f32[144,256]{1,0:T(8,128)S(1)}, f32[144,256]{1,0:T(8,128)S(1)}, u32[]{:S(2)}, u32[]{:S(2)}) collective-permute-start(f32[144,256]{1,0:T(8,128)S(1)} %shard_map.107.mine_ref), channel_id=1, source_target_pairs={{0,32},{32,0},{1,33},{33,1},{2,34},{34,2},{3,35},{35,3},{4,36},{36... | collective-permute-start | bytes 442376 | tf_op jit(solution)/shard_map/ppermute | solution.py:362
  (55 shorter events, 13.9 us)
Async XLA Ops:
  7.2 45.1 %all-gather.2.cloned.1.call-start = ((), (), s32[]{:S(2)}) async-start(), calls=%async_computation | async-start | bytes 2654208 | tf_op jit(solution)/shard_map/all_gather | solution.py:388
  10.8 41.4 %copy-start = (bf16[256,4608]{1,0:T(8,128)(2,1)S(1)}, bf16[256,4608]{1,0:T(8,128)(2,1)}, u32[]{:S(2)}) copy-start(bf16[256,4608]{1,0:T(8,128)(2,1)} %own_ref.3) | copy-start | bytes 7077892
  10.9 27.4 %collective-permute-start = (bf16[256,2176]{1,0:T(8,128)(2,1)}, bf16[256,2176]{1,0:T(8,128)(2,1)}, u32[]{:S(2)}, u32[]{:S(2)}) collective-permute-start(bf16[256,2176]{1,0:T(8,128)(2,1)} %shard_map.94), channel_id=1, source_target_pairs={{0,16},{8,24},{16,0},{24,8},{1,17},{9,25},{17,1},{25,9},{2,18},{10... | collective-permute-start | bytes 3342344 | tf_op jit(solution)/shard_map/ppermute | solution.py:362
  17.4 45.9 %collective-permute-start.2 = (bf16[256,2176]{1,0:T(8,128)(2,1)}, bf16[256,2176]{1,0:T(8,128)(2,1)}, u32[]{:S(2)}, u32[]{:S(2)}) collective-permute-start(bf16[256,2176]{1,0:T(8,128)(2,1)} %get-tuple-element.29), channel_id=1, source_target_pairs={{0,8},{8,0},{16,24},{24,16},{1,9},{9,1},{17,25},{25,17},{2,10},{10... | collective-permute-start | bytes 3342344 | tf_op jit(solution)/shard_map/ppermute | solution.py:362
  17.9 46.0 %collective-permute-start.3 = (bf16[256,2176]{1,0:T(8,128)(2,1)}, bf16[256,2176]{1,0:T(8,128)(2,1)}, u32[]{:S(2)}, u32[]{:S(2)}) collective-permute-start(bf16[256,2176]{1,0:T(8,128)(2,1)} %get-tuple-element.30), channel_id=1, source_target_pairs={{0,24},{8,16},{16,8},{24,0},{1,25},{9,17},{17,9},{25,1},{2,26},{10... | collective-permute-start | bytes 3342344 | tf_op jit(solution)/shard_map/ppermute | solution.py:362
  67.4 13.3 %collective-permute-start.6 = (bf16[4,144,512]{2,1,0:T(8,128)(2,1)S(1)}, bf16[4,144,512]{2,1,0:T(8,128)(2,1)S(1)}, u32[]{:S(2)}, u32[]{:S(2)}) collective-permute-start(bf16[4,144,512]{2,1,0:T(8,128)(2,1)S(1)} %get-tuple-element.35), channel_id=1, source_target_pairs={{0,1},{1,0},{2,3},{3,2},{4,5},{5,4},{6,7},{7,6},{32,39},{33,34},{3... | collective-permute-start | bytes 1769480 | tf_op jit(solution)/shard_map/ppermute | solution.py:371
  73.1 17.1 %collective-permute-start.9 = (bf16[4,144,512]{2,1,0:T(8,128)(2,1)S(1)}, bf16[4,144,512]{2,1,0:T(8,128)(2,1)S(1)}, u32[]{:S(2)}, u32[]{:S(2)}) collective-permute-start(bf16[4,144,512]{2,1,0:T(8,128)(2,1)S(1)} %get-tuple-element.41), channel_id=1, source_target_pairs={{0,1},{1,0},{2,3},{3,2},{4,5},{5,4},{6,7},{7,6},{32,39},{33,34},{3... | collective-permute-start | bytes 1769480 | tf_op jit(solution)/shard_map/ppermute | solution.py:371
  73.2 12.8 %collective-permute-start.1 = (bf16[256,1024]{1,0:T(8,128)(2,1)S(1)}, bf16[256,1024]{1,0:T(8,128)(2,1)S(1)}, u32[]{:S(2)}, u32[]{:S(2)}) collective-permute-start(bf16[256,1024]{1,0:T(8,128)(2,1)S(1)} %get-tuple-element.28.refs_0_), channel_id=1, source_target_pairs={{0,16},{8,24},{16,0},{24,8},{1,17},{9,25},{17,1},{25,9},{2,18},{10... | collective-permute-start | bytes 1572872 | tf_op jit(solution)/shard_map/ppermute | solution.py:362
  80.8 14.1 %collective-permute-start.7 = (bf16[2,144,512]{2,1,0:T(8,128)(2,1)S(1)}, bf16[2,144,512]{2,1,0:T(8,128)(2,1)S(1)}, u32[]{:S(2)}, u32[]{:S(2)}) collective-permute-start(bf16[2,144,512]{2,1,0:T(8,128)(2,1)S(1)} %get-tuple-element.37), channel_id=1, source_target_pairs={{0,6},{1,3},{2,0},{3,5},{4,2},{5,7},{6,4},{7,1},{32,34},{33,39},{3... | collective-permute-start | bytes 884744 | tf_op jit(solution)/shard_map/ppermute | solution.py:371
  90.3 13.3 %copy-start.4 = (f32[1,144,1024]{2,1,0:T(8,128)S(1)}, f32[1,144,1024]{2,1,0:T(8,128)}, u32[]{:S(2)}) copy-start(f32[1,144,1024]{2,1,0:T(8,128)} %param.10) | copy-start | bytes 1769476
  90.3 13.3 %copy-start.6 = (f32[256,128]{1,0:T(8,128)S(1)}, f32[256,128]{1,0:T(8,128)}, u32[]{:S(2)}) copy-start(f32[256,128]{1,0:T(8,128)} %constant.32.clone.table_ref) | copy-start | bytes 393220
  90.3 8.4 %collective-permute-start.10 = (bf16[2,144,512]{2,1,0:T(8,128)(2,1)S(1)}, bf16[2,144,512]{2,1,0:T(8,128)(2,1)S(1)}, u32[]{:S(2)}, u32[]{:S(2)}) collective-permute-start(bf16[2,144,512]{2,1,0:T(8,128)(2,1)S(1)} %get-tuple-element.43), channel_id=1, source_target_pairs={{0,6},{1,3},{2,0},{3,5},{4,2},{5,7},{6,4},{7,1},{32,34},{33,39},{3... | collective-permute-start | bytes 884744 | tf_op jit(solution)/shard_map/ppermute | solution.py:371
  90.4 16.8 %collective-permute-start.4 = (bf16[256,1024]{1,0:T(8,128)(2,1)S(1)}, bf16[256,1024]{1,0:T(8,128)(2,1)S(1)}, u32[]{:S(2)}, u32[]{:S(2)}) collective-permute-start(bf16[256,1024]{1,0:T(8,128)(2,1)S(1)} %get-tuple-element.31.rest_0_), channel_id=1, source_target_pairs={{0,8},{8,0},{16,24},{24,16},{1,9},{9,1},{17,25},{25,17},{2,10},{10... | collective-permute-start | bytes 1572872 | tf_op jit(solution)/shard_map/ppermute | solution.py:362
  92.1 15.4 %collective-permute-start.5 = (bf16[256,1024]{1,0:T(8,128)(2,1)S(1)}, bf16[256,1024]{1,0:T(8,128)(2,1)S(1)}, u32[]{:S(2)}, u32[]{:S(2)}) collective-permute-start(bf16[256,1024]{1,0:T(8,128)(2,1)S(1)} %get-tuple-element.32.rest_1_), channel_id=1, source_target_pairs={{0,24},{8,16},{16,8},{24,0},{1,25},{9,17},{17,9},{25,1},{2,26},{10... | collective-permute-start | bytes 1572872 | tf_op jit(solution)/shard_map/ppermute | solution.py:362
  95.0 8.7 %collective-permute-start.8 = (bf16[144,512]{1,0:T(8,128)(2,1)S(1)}, bf16[144,512]{1,0:T(8,128)(2,1)S(1)}, u32[]{:S(2)}, u32[]{:S(2)}) collective-permute-start(bf16[144,512]{1,0:T(8,128)(2,1)S(1)} %fusion), channel_id=1, source_target_pairs={{0,7},{1,2},{2,1},{3,4},{4,3},{5,6},{6,5},{7,0},{32,33},{33,32},{3... | collective-permute-start | bytes 442376 | tf_op jit(solution)/shard_map/ppermute | solution.py:371
  98.7 8.7 %collective-permute-start.11 = (bf16[144,512]{1,0:T(8,128)(2,1)S(1)}, bf16[144,512]{1,0:T(8,128)(2,1)S(1)}, u32[]{:S(2)}, u32[]{:S(2)}) collective-permute-start(bf16[144,512]{1,0:T(8,128)(2,1)S(1)} %fusion.1), channel_id=1, source_target_pairs={{0,7},{1,2},{2,1},{3,4},{4,3},{5,6},{6,5},{7,0},{32,33},{33,32},{3... | collective-permute-start | bytes 442376 | tf_op jit(solution)/shard_map/ppermute | solution.py:371
  104.1 6.9 %collective-permute-start.18 = (bf16[144,256]{1,0:T(8,128)(2,1)S(1)}, bf16[144,256]{1,0:T(8,128)(2,1)S(1)}, u32[]{:S(2)}, u32[]{:S(2)}) collective-permute-start(bf16[144,256]{1,0:T(8,128)(2,1)S(1)} %get-tuple-element.50.refs_0_), channel_id=1, source_target_pairs={{0,192},{64,128},{128,64},{192,0},{1,193},{65,129},{129,65},{193,1... | collective-permute-start | bytes 221192 | tf_op jit(solution)/shard_map/ppermute | solution.py:362
  106.7 7.1 %collective-permute-start.17 = (bf16[144,256]{1,0:T(8,128)(2,1)S(1)}, bf16[144,256]{1,0:T(8,128)(2,1)S(1)}, u32[]{:S(2)}, u32[]{:S(2)}) collective-permute-start(bf16[144,256]{1,0:T(8,128)(2,1)S(1)} %get-tuple-element.50.refs_0_), channel_id=1, source_target_pairs={{0,128},{64,192},{128,0},{192,64},{1,129},{65,193},{129,1},{193,65... | collective-permute-start | bytes 221192 | tf_op jit(solution)/shard_map/ppermute | solution.py:362
  107.2 6.6 %collective-permute-start.16 = (bf16[144,256]{1,0:T(8,128)(2,1)S(1)}, bf16[144,256]{1,0:T(8,128)(2,1)S(1)}, u32[]{:S(2)}, u32[]{:S(2)}) collective-permute-start(bf16[144,256]{1,0:T(8,128)(2,1)S(1)} %get-tuple-element.50.refs_0_), channel_id=1, source_target_pairs={{0,64},{64,0},{128,192},{192,128},{1,65},{65,1},{129,193},{193,129... | collective-permute-start | bytes 221192 | tf_op jit(solution)/shard_map/ppermute | solution.py:362
  108.0 9.8 %collective-permute-start.14 = (bf16[144,256]{1,0:T(8,128)(2,1)S(1)}, bf16[144,256]{1,0:T(8,128)(2,1)S(1)}, u32[]{:S(2)}, u32[]{:S(2)}) collective-permute-start(bf16[144,256]{1,0:T(8,128)(2,1)S(1)} %get-tuple-element.47.refs_0_), channel_id=1, source_target_pairs={{0,192},{64,128},{128,64},{192,0},{1,193},{65,129},{129,65},{193,1... | collective-permute-start | bytes 221192 | tf_op jit(solution)/shard_map/ppermute | solution.py:362
  110.5 7.3 %collective-permute-start.13 = (bf16[144,256]{1,0:T(8,128)(2,1)S(1)}, bf16[144,256]{1,0:T(8,128)(2,1)S(1)}, u32[]{:S(2)}, u32[]{:S(2)}) collective-permute-start(bf16[144,256]{1,0:T(8,128)(2,1)S(1)} %get-tuple-element.47.refs_0_), channel_id=1, source_target_pairs={{0,128},{64,192},{128,0},{192,64},{1,129},{65,193},{129,1},{193,65... | collective-permute-start | bytes 221192 | tf_op jit(solution)/shard_map/ppermute | solution.py:362
  111.0 6.7 %collective-permute-start.12 = (bf16[144,256]{1,0:T(8,128)(2,1)S(1)}, bf16[144,256]{1,0:T(8,128)(2,1)S(1)}, u32[]{:S(2)}, u32[]{:S(2)}) collective-permute-start(bf16[144,256]{1,0:T(8,128)(2,1)S(1)} %get-tuple-element.47.refs_0_), channel_id=1, source_target_pairs={{0,64},{64,0},{128,192},{192,128},{1,65},{65,1},{129,193},{193,129... | collective-permute-start | bytes 221192 | tf_op jit(solution)/shard_map/ppermute | solution.py:362
  113.8 6.0 %collective-permute-start.19 = (f32[144,256]{1,0:T(8,128)S(1)}, f32[144,256]{1,0:T(8,128)S(1)}, u32[]{:S(2)}, u32[]{:S(2)}) collective-permute-start(f32[144,256]{1,0:T(8,128)S(1)} %shard_map.108.mine_ref), channel_id=1, source_target_pairs={{0,32},{32,0},{1,33},{33,1},{2,34},{34,2},{3,35},{35,3},{4,36},{36... | collective-permute-start | bytes 442376 | tf_op jit(solution)/shard_map/ppermute | solution.py:362
  117.8 3.1 %collective-permute-start.15 = (f32[144,256]{1,0:T(8,128)S(1)}, f32[144,256]{1,0:T(8,128)S(1)}, u32[]{:S(2)}, u32[]{:S(2)}) collective-permute-start(f32[144,256]{1,0:T(8,128)S(1)} %shard_map.107.mine_ref), channel_id=1, source_target_pairs={{0,32},{32,0},{1,33},{33,1},{2,34},{34,2},{3,35},{35,3},{4,36},{36... | collective-permute-start | bytes 442376 | tf_op jit(solution)/shard_map/ppermute | solution.py:362
  (5 other events, 25.3 us)
Sparse Core Ops, SparseCore 0:
  9.8 42.4 all-gather.1

commit v3 on v2

--- a/solution.py
+++ b/solution.py
@@ -53,13 +53,16 @@
         copy = pltpu.make_async_copy(tok_ref.at[:, pl.ds(start, width)], bufs[i].at[:, :width], in_sems.at[i])
         copy.start()
         in_copies.append(copy)
-        out_copies.append(pltpu.make_async_copy(bufs[i], outs[i], out_sems.at[i]))
+        for j, part in enumerate((pl.ds(0, width), pl.ds(width, cot_ref.shape[1]))):
+            copy = pltpu.make_async_copy(bufs[i].at[:, part], outs[i].at[:, part], out_sems.at[2 * i + j])
+            out_copies.append(copy)
     cot_copy.wait()
     masked = mask_rows(cot_buffer[...], length_ref[0])
-    for buf, in_copy, out_copy in zip(bufs, in_copies, out_copies):
+    for i, buf in enumerate(bufs):
         buf[:, width:] = masked
-        in_copy.wait()
-        out_copy.start()
+        out_copies[2 * i + 1].start()
+        in_copies[i].wait()
+        out_copies[2 * i].start()
     for copy in out_copies:
         copy.wait()
 
@@ -77,7 +80,7 @@
         + [
             pltpu.VMEM(cotangent.shape, BF16),
             pltpu.SemaphoreType.DMA((count + 1,)),
-            pltpu.SemaphoreType.DMA((count,)),
+            pltpu.SemaphoreType.DMA((2 * count,)),
         ],
         compiler_params=ALL,
     )(y, lengths, tokens, cotangent)

time: 129 us -> 129 us (level)
  no operation moved by 1% of the time
where the time goes in v3:
time: 129 us
  waiting for transfers between devices  51.3 us (40%)
  starting transfers between devices  36.5 us (28%)
  Pallas kernels  24.2 us (19%)
  between operations  14.8 us (11%)
  local copies, waits for them, and re-layouts  1.7 us (1%)
    ppermute x14, waiting for transfers between devices, swap(): lax.ppermute(array, axis, [(i, i ^ d) for i in range(lax.axis_size(axis))])  27.9 us
    ppermute x14, starting transfers between devices, swap(): lax.ppermute(array, axis, [(i, i ^ d) for i in range(lax.axis_size(axis))])  24 us
    all_gather x1, waiting for transfers between devices, per_device(): weight_quarter = lax.all_gather(weight, 'z', axis=0, tiled=True)  14.1 us
    ppermute x6, starting transfers between devices, move(): lax.ppermute(array, ('core', 'z'), [(c * nz + z, c * nz + (z + steps * si...  12.4 us
    ppermute x6, waiting for transfers between devices, move(): lax.ppermute(array, ('core', 'z'), [(c * nz + z, c * nz + (z + steps * si...  8.59 us
    pallas_call x2, Pallas kernels, split_inputs(): pl.pallas_call(functools.partial(split_kernel, order), out_shape=[jax.Sha...  4.73 us
    pallas_call x1, Pallas kernels, grad_terms(): pl.pallas_call(functools.partial(grad_kernel, nz, len(after)), out_shape=...  3.44 us
    pallas_call x1, Pallas kernels, project_rest(): pl.pallas_call(project_kernel, out_shape=[shape, shape], in_specs=[VMEM]...  3.13 us
  transfers between devices with their start and end apart: 21, of which 10 were waited for; matrix products, arithmetic and copies ran while one was open for 0% of the time, Pallas kernels for 15%

profile of v3, /device:TPU:1, one launch (start us, length us, event | category | flops | bytes accessed | tf_op | source)
XLA Modules:
  0.0 128.7 jit_solution(18145558610152755595)
XLA Ops:
  8.5 2.1 %shard_map.94 = bf16[256,2176]{1,0:T(8,128)(2,1)} custom-call(s32[1]{0:T(128)} %bitcast.y_ref, s32[1]{0:T(128)S(6)} %copy.12.length_ref, bf16[256,4608]{1,0:T(8,128)(2,1)} %own_ref.3, bf16[256,1024]{1,0:T(8,128)(2,1)} %cot_ref.5), custom_call_target="tpu_custom_call" | custom-call | tf_op jit(solution)/shard_map/pallas_call | solution.py:74
  10.7 3.8 %collective-permute-start = (bf16[256,2176]{1,0:T(8,128)(2,1)}, bf16[256,2176]{1,0:T(8,128)(2,1)}, u32[]{:S(2)}, u32[]{:S(2)}) collective-permute-start(bf16[256,2176]{1,0:T(8,128)(2,1)} %shard_map.94), channel_id=1, source_target_pairs={{0,16},{8,24},{16,0},{24,8},{1,17},{9,25},{17,1},{25,9},{2,18},{10... | collective-permute-start | bytes 3342344 | tf_op jit(solution)/shard_map/ppermute | solution.py:365
  14.6 2.6 %shard_map.96 = (bf16[256,2176]{1,0:T(8,128)(2,1)}, bf16[256,2176]{1,0:T(8,128)(2,1)}) custom-call(s32[1]{0:T(128)} %bitcast.y_ref, s32[1]{0:T(128)S(6)} %copy.12.length_ref, bf16[256,4608]{1,0:T(8,128)(2,1)} %own_ref.3, bf16[256,1024]{1,0:T(8,128)(2,1)} %cot_ref.5), custom_call_target="tpu_custom_call" | custom-call | tf_op jit(solution)/shard_map/pallas_call | solution.py:74
  19.6 18.5 %collective-permute-done.both_ref = bf16[256,2176]{1,0:T(8,128)(2,1)} collective-permute-done((bf16[256,2176]{1,0:T(8,128)(2,1)}, bf16[256,2176]{1,0:T(8,128)(2,1)}, u32[]{:S(2)}, u32[]{:S(2)}) %collective-permute-start) | collective-permute-done | bytes 1114144 | tf_op jit(solution)/shard_map/ppermute | solution.py:365
  38.2 14.1 %all-gather.2.cloned.1.call-done.weight_ref.after_ref = bf16[1152,1024]{1,0:T(8,128)(2,1)} async-done(((bf16[144,1024]{1,0:T(8,128)(2,1)}), bf16[1152,1024]{1,0:T(8,128)(2,1)}) %all-gather.2.cloned.1.call-update) | async-done | bytes 2359312 | tf_op jit(solution)/shard_map/all_gather | solution.py:391
  52.3 1.7 %copy-done.1 = bf16[1152,1024]{1,0:T(8,128)(2,1)S(1)} copy-done((bf16[1152,1024]{1,0:T(8,128)(2,1)S(1)}, bf16[1152,1024]{1,0:T(8,128)(2,1)}, u32[]{:S(2)}) %copy-start.1) | copy-done | bytes 2359320
  53.9 2.9 %shard_map.95 = (f32[256,1024]{1,0:T(8,128)S(1)}, bf16[256,1024]{1,0:T(8,128)(2,1)S(1)}) custom-call(s32[1]{0:T(128)} %bitcast.y_ref, bf16[256,4608]{1,0:T(8,128)(2,1)S(1)} %copy-done, bf16[256,2176]{1,0:T(8,128)(2,1)} %collective-permute-done.both_ref, bf16[1152,1024]{1,0:T(8,128)(2,1)S(1)} %copy-done.1), custom_call_target="tpu_custom_call" | custom-call | tf_op jit(solution)/shard_map/pallas_call | solution.py:188
  56.8 2.7 %shard_map.100.first_ref = f32[1152,1024]{1,0:T(8,128)S(1)} custom-call(s32[1]{0:T(128)} %bitcast.y_ref, s32[1]{0:T(128)S(6)} %copy.12.length_ref, bf16[256,4608]{1,0:T(8,128)(2,1)S(1)} %copy-done, bf16[256,1024]{1,0:T(8,128)(2,1)S(1)} %copy-done.3, bf16[256,2176]{1,0:T(8,128)(2,1)} %collective-permute-done.both_ref, bf16[1152,1024]{1,0:T(8,128)(2,1)S(1)} %copy-done.1), custom_call_target="tpu_custom_call" | custom-call | tf_op jit(solution)/shard_map/pallas_call | solution.py:109
  59.5 3.6 %collective-permute-done.2.one_ref = bf16[256,2176]{1,0:T(8,128)(2,1)} collective-permute-done((bf16[256,2176]{1,0:T(8,128)(2,1)}, bf16[256,2176]{1,0:T(8,128)(2,1)}, u32[]{:S(2)}, u32[]{:S(2)}) %collective-permute-start.2) | collective-permute-done | bytes 1114144 | tf_op jit(solution)/shard_map/ppermute | solution.py:365
  63.8 3.4 %shard_map.101 = (f32[4,144,512]{2,1,0:T(8,128)S(1)}, bf16[4,144,512]{2,1,0:T(8,128)(2,1)S(1)}, f32[4,144,512]{2,1,0:T(8,128)S(1)}, bf16[4,144,512]{2,1,0:T(8,128)(2,1)S(1)}) custom-call(s32[2]{0:T(128)S(1)} %pad_add_fusion.place_ref, f32[1152,1024]{1,0:T(8,128)S(1)} %shard_map.100.first_ref, bf16[256,2176]{1,0:T(8,128)(2,1)} %collective-permute-done.2.one_ref, ...), custom_call_target="tpu_custom_call" | custom-call | tf_op jit(solution)/shard_map/pallas_call | solution.py:152
  67.2 5.7 %collective-permute-start.6 = (bf16[4,144,512]{2,1,0:T(8,128)(2,1)S(1)}, bf16[4,144,512]{2,1,0:T(8,128)(2,1)S(1)}, u32[]{:S(2)}, u32[]{:S(2)}) collective-permute-start(bf16[4,144,512]{2,1,0:T(8,128)(2,1)S(1)} %get-tuple-element.35), channel_id=1, source_target_pairs={{0,1},{1,0},{2,3},{3,2},{4,5},{5,4},{6,7},{7,6},{32,39},{33,34},{3... | collective-permute-start | bytes 1769480 | tf_op jit(solution)/shard_map/ppermute | solution.py:374
  73.0 2.9 %collective-permute-start.1 = (bf16[256,1024]{1,0:T(8,128)(2,1)S(1)}, bf16[256,1024]{1,0:T(8,128)(2,1)S(1)}, u32[]{:S(2)}, u32[]{:S(2)}) collective-permute-start(bf16[256,1024]{1,0:T(8,128)(2,1)S(1)} %get-tuple-element.28.refs_0_), channel_id=1, source_target_pairs={{0,16},{8,24},{16,0},{24,8},{1,17},{9,25},{17,1},{25,9},{2,18},{10... | collective-permute-start | bytes 1572872 | tf_op jit(solution)/shard_map/ppermute | solution.py:365
  76.0 3.1 %shard_map.97 = (bf16[256,1024]{1,0:T(8,128)(2,1)S(1)}, bf16[256,1024]{1,0:T(8,128)(2,1)S(1)}) custom-call(bf16[256,2176]{1,0:T(8,128)(2,1)} %collective-permute-done.2.one_ref, bf16[256,2176]{1,0:T(8,128)(2,1)} %collective-permute-done.3.two_ref, bf16[1152,1024]{1,0:T(8,128)(2,1)S(1)} %copy-done.2), custom_call_target="tpu_custom_call" | custom-call | tf_op jit(solution)/shard_map/pallas_call | solution.py:209
  80.7 5.2 %collective-permute-done.1.one_ref.rest_0_ = bf16[256,1024]{1,0:T(8,128)(2,1)S(1)} collective-permute-done((bf16[256,1024]{1,0:T(8,128)(2,1)S(1)}, bf16[256,1024]{1,0:T(8,128)(2,1)S(1)}, u32[]{:S(2)}, u32[]{:S(2)}) %collective-permute-start.1) | collective-permute-done | bytes 524320 | tf_op jit(solution)/shard_map/ppermute | solution.py:365
  85.9 4.2 %collective-permute-done.9.got_ref = bf16[4,144,512]{2,1,0:T(8,128)(2,1)S(1)} collective-permute-done((bf16[4,144,512]{2,1,0:T(8,128)(2,1)S(1)}, bf16[4,144,512]{2,1,0:T(8,128)(2,1)S(1)}, u32[]{:S(2)}, u32[]{:S(2)}) %collective-permute-start.9) | collective-permute-done | bytes 589856 | tf_op jit(solution)/shard_map/ppermute | solution.py:374
  90.3 1.7 %collective-permute-start.4 = (bf16[256,1024]{1,0:T(8,128)(2,1)S(1)}, bf16[256,1024]{1,0:T(8,128)(2,1)S(1)}, u32[]{:S(2)}, u32[]{:S(2)}) collective-permute-start(bf16[256,1024]{1,0:T(8,128)(2,1)S(1)} %get-tuple-element.31.rest_0_), channel_id=1, source_target_pairs={{0,8},{8,0},{16,24},{24,16},{1,9},{9,1},{17,25},{25,17},{2,10},{10... | collective-permute-start | bytes 1572872 | tf_op jit(solution)/shard_map/ppermute | solution.py:365
  92.0 2.1 %collective-permute-start.5 = (bf16[256,1024]{1,0:T(8,128)(2,1)S(1)}, bf16[256,1024]{1,0:T(8,128)(2,1)S(1)}, u32[]{:S(2)}, u32[]{:S(2)}) collective-permute-start(bf16[256,1024]{1,0:T(8,128)(2,1)S(1)} %get-tuple-element.32.rest_1_), channel_id=1, source_target_pairs={{0,24},{8,16},{16,8},{24,0},{1,25},{9,17},{17,9},{25,1},{2,26},{10... | collective-permute-start | bytes 1572872 | tf_op jit(solution)/shard_map/ppermute | solution.py:365
  94.8 3.7 %collective-permute-start.8 = (bf16[144,512]{1,0:T(8,128)(2,1)S(1)}, bf16[144,512]{1,0:T(8,128)(2,1)S(1)}, u32[]{:S(2)}, u32[]{:S(2)}) collective-permute-start(bf16[144,512]{1,0:T(8,128)(2,1)S(1)} %fusion), channel_id=1, source_target_pairs={{0,7},{1,2},{2,1},{3,4},{4,3},{5,6},{6,5},{7,0},{32,33},{33,32},{3... | collective-permute-start | bytes 442376 | tf_op jit(solution)/shard_map/ppermute | solution.py:374
  98.6 2.7 %collective-permute-start.11 = (bf16[144,512]{1,0:T(8,128)(2,1)S(1)}, bf16[144,512]{1,0:T(8,128)(2,1)S(1)}, u32[]{:S(2)}, u32[]{:S(2)}) collective-permute-start(bf16[144,512]{1,0:T(8,128)(2,1)S(1)} %fusion.1), channel_id=1, source_target_pairs={{0,7},{1,2},{2,1},{3,4},{4,3},{5,6},{6,5},{7,0},{32,33},{33,32},{3... | collective-permute-start | bytes 442376 | tf_op jit(solution)/shard_map/ppermute | solution.py:374
  101.3 2.2 %collective-permute-done.8.last_ref = bf16[144,512]{1,0:T(8,128)(2,1)S(1)} collective-permute-done((bf16[144,512]{1,0:T(8,128)(2,1)S(1)}, bf16[144,512]{1,0:T(8,128)(2,1)S(1)}, u32[]{:S(2)}, u32[]{:S(2)}) %collective-permute-start.8) | collective-permute-done | bytes 147488 | tf_op jit(solution)/shard_map/ppermute | solution.py:374
  104.0 2.6 %collective-permute-start.18 = (bf16[144,256]{1,0:T(8,128)(2,1)S(1)}, bf16[144,256]{1,0:T(8,128)(2,1)S(1)}, u32[]{:S(2)}, u32[]{:S(2)}) collective-permute-start(bf16[144,256]{1,0:T(8,128)(2,1)S(1)} %get-tuple-element.50.refs_0_), channel_id=1, source_target_pairs={{0,192},{64,128},{128,64},{192,0},{1,193},{65,129},{129,65},{193,1... | collective-permute-start | bytes 221192 | tf_op jit(solution)/shard_map/ppermute | solution.py:365
  107.8 2.6 %collective-permute-start.14 = (bf16[144,256]{1,0:T(8,128)(2,1)S(1)}, bf16[144,256]{1,0:T(8,128)(2,1)S(1)}, u32[]{:S(2)}, u32[]{:S(2)}) collective-permute-start(bf16[144,256]{1,0:T(8,128)(2,1)S(1)} %get-tuple-element.47.refs_0_), channel_id=1, source_target_pairs={{0,192},{64,128},{128,64},{192,0},{1,193},{65,129},{129,65},{193,1... | collective-permute-start | bytes 221192 | tf_op jit(solution)/shard_map/ppermute | solution.py:365
  113.7 3.9 %collective-permute-start.19 = (f32[144,256]{1,0:T(8,128)S(1)}, f32[144,256]{1,0:T(8,128)S(1)}, u32[]{:S(2)}, u32[]{:S(2)}) collective-permute-start(f32[144,256]{1,0:T(8,128)S(1)} %shard_map.108.mine_ref), channel_id=1, source_target_pairs={{0,32},{32,0},{1,33},{33,1},{2,34},{34,2},{3,35},{35,3},{4,36},{36... | collective-permute-start | bytes 442376 | tf_op jit(solution)/shard_map/ppermute | solution.py:365
  117.7 2.0 %collective-permute-start.15 = (f32[144,256]{1,0:T(8,128)S(1)}, f32[144,256]{1,0:T(8,128)S(1)}, u32[]{:S(2)}, u32[]{:S(2)}) collective-permute-start(f32[144,256]{1,0:T(8,128)S(1)} %shard_map.107.mine_ref), channel_id=1, source_target_pairs={{0,32},{32,0},{1,33},{33,1},{2,34},{34,2},{3,35},{35,3},{4,36},{36... | collective-permute-start | bytes 442376 | tf_op jit(solution)/shard_map/ppermute | solution.py:365
  (55 shorter events, 13.9 us)
Async XLA Ops:
  7.2 45.1 %all-gather.2.cloned.1.call-start = ((), (), s32[]{:S(2)}) async-start(), calls=%async_computation | async-start | bytes 2654208 | tf_op jit(solution)/shard_map/all_gather | solution.py:391
  10.7 41.5 %copy-start = (bf16[256,4608]{1,0:T(8,128)(2,1)S(1)}, bf16[256,4608]{1,0:T(8,128)(2,1)}, u32[]{:S(2)}) copy-start(bf16[256,4608]{1,0:T(8,128)(2,1)} %own_ref.3) | copy-start | bytes 7077892
  10.7 27.4 %collective-permute-start = (bf16[256,2176]{1,0:T(8,128)(2,1)}, bf16[256,2176]{1,0:T(8,128)(2,1)}, u32[]{:S(2)}, u32[]{:S(2)}) collective-permute-start(bf16[256,2176]{1,0:T(8,128)(2,1)} %shard_map.94), channel_id=1, source_target_pairs={{0,16},{8,24},{16,0},{24,8},{1,17},{9,25},{17,1},{25,9},{2,18},{10... | collective-permute-start | bytes 3342344 | tf_op jit(solution)/shard_map/ppermute | solution.py:365
  17.1 46.0 %collective-permute-start.2 = (bf16[256,2176]{1,0:T(8,128)(2,1)}, bf16[256,2176]{1,0:T(8,128)(2,1)}, u32[]{:S(2)}, u32[]{:S(2)}) collective-permute-start(bf16[256,2176]{1,0:T(8,128)(2,1)} %get-tuple-element.29), channel_id=1, source_target_pairs={{0,8},{8,0},{16,24},{24,16},{1,9},{9,1},{17,25},{25,17},{2,10},{10... | collective-permute-start | bytes 3342344 | tf_op jit(solution)/shard_map/ppermute | solution.py:365
  17.6 46.1 %collective-permute-start.3 = (bf16[256,2176]{1,0:T(8,128)(2,1)}, bf16[256,2176]{1,0:T(8,128)(2,1)}, u32[]{:S(2)}, u32[]{:S(2)}) collective-permute-start(bf16[256,2176]{1,0:T(8,128)(2,1)} %get-tuple-element.30), channel_id=1, source_target_pairs={{0,24},{8,16},{16,8},{24,0},{1,25},{9,17},{17,9},{25,1},{2,26},{10... | collective-permute-start | bytes 3342344 | tf_op jit(solution)/shard_map/ppermute | solution.py:365
  67.2 13.3 %collective-permute-start.6 = (bf16[4,144,512]{2,1,0:T(8,128)(2,1)S(1)}, bf16[4,144,512]{2,1,0:T(8,128)(2,1)S(1)}, u32[]{:S(2)}, u32[]{:S(2)}) collective-permute-start(bf16[4,144,512]{2,1,0:T(8,128)(2,1)S(1)} %get-tuple-element.35), channel_id=1, source_target_pairs={{0,1},{1,0},{2,3},{3,2},{4,5},{5,4},{6,7},{7,6},{32,39},{33,34},{3... | collective-permute-start | bytes 1769480 | tf_op jit(solution)/shard_map/ppermute | solution.py:374
  72.9 17.1 %collective-permute-start.9 = (bf16[4,144,512]{2,1,0:T(8,128)(2,1)S(1)}, bf16[4,144,512]{2,1,0:T(8,128)(2,1)S(1)}, u32[]{:S(2)}, u32[]{:S(2)}) collective-permute-start(bf16[4,144,512]{2,1,0:T(8,128)(2,1)S(1)} %get-tuple-element.41), channel_id=1, source_target_pairs={{0,1},{1,0},{2,3},{3,2},{4,5},{5,4},{6,7},{7,6},{32,39},{33,34},{3... | collective-permute-start | bytes 1769480 | tf_op jit(solution)/shard_map/ppermute | solution.py:374
  73.0 12.8 %collective-permute-start.1 = (bf16[256,1024]{1,0:T(8,128)(2,1)S(1)}, bf16[256,1024]{1,0:T(8,128)(2,1)S(1)}, u32[]{:S(2)}, u32[]{:S(2)}) collective-permute-start(bf16[256,1024]{1,0:T(8,128)(2,1)S(1)} %get-tuple-element.28.refs_0_), channel_id=1, source_target_pairs={{0,16},{8,24},{16,0},{24,8},{1,17},{9,25},{17,1},{25,9},{2,18},{10... | collective-permute-start | bytes 1572872 | tf_op jit(solution)/shard_map/ppermute | solution.py:365
  80.6 14.1 %collective-permute-start.7 = (bf16[2,144,512]{2,1,0:T(8,128)(2,1)S(1)}, bf16[2,144,512]{2,1,0:T(8,128)(2,1)S(1)}, u32[]{:S(2)}, u32[]{:S(2)}) collective-permute-start(bf16[2,144,512]{2,1,0:T(8,128)(2,1)S(1)} %get-tuple-element.37), channel_id=1, source_target_pairs={{0,6},{1,3},{2,0},{3,5},{4,2},{5,7},{6,4},{7,1},{32,34},{33,39},{3... | collective-permute-start | bytes 884744 | tf_op jit(solution)/shard_map/ppermute | solution.py:374
  90.2 13.3 %copy-start.4 = (f32[1,144,1024]{2,1,0:T(8,128)S(1)}, f32[1,144,1024]{2,1,0:T(8,128)}, u32[]{:S(2)}) copy-start(f32[1,144,1024]{2,1,0:T(8,128)} %param.10) | copy-start | bytes 1769476
  90.2 13.3 %copy-start.6 = (f32[256,128]{1,0:T(8,128)S(1)}, f32[256,128]{1,0:T(8,128)}, u32[]{:S(2)}) copy-start(f32[256,128]{1,0:T(8,128)} %constant.32.clone.table_ref) | copy-start | bytes 393220
  90.2 8.4 %collective-permute-start.10 = (bf16[2,144,512]{2,1,0:T(8,128)(2,1)S(1)}, bf16[2,144,512]{2,1,0:T(8,128)(2,1)S(1)}, u32[]{:S(2)}, u32[]{:S(2)}) collective-permute-start(bf16[2,144,512]{2,1,0:T(8,128)(2,1)S(1)} %get-tuple-element.43), channel_id=1, source_target_pairs={{0,6},{1,3},{2,0},{3,5},{4,2},{5,7},{6,4},{7,1},{32,34},{33,39},{3... | collective-permute-start | bytes 884744 | tf_op jit(solution)/shard_map/ppermute | solution.py:374
  90.3 16.8 %collective-permute-start.4 = (bf16[256,1024]{1,0:T(8,128)(2,1)S(1)}, bf16[256,1024]{1,0:T(8,128)(2,1)S(1)}, u32[]{:S(2)}, u32[]{:S(2)}) collective-permute-start(bf16[256,1024]{1,0:T(8,128)(2,1)S(1)} %get-tuple-element.31.rest_0_), channel_id=1, source_target_pairs={{0,8},{8,0},{16,24},{24,16},{1,9},{9,1},{17,25},{25,17},{2,10},{10... | collective-permute-start | bytes 1572872 | tf_op jit(solution)/shard_map/ppermute | solution.py:365
  92.0 15.4 %collective-permute-start.5 = (bf16[256,1024]{1,0:T(8,128)(2,1)S(1)}, bf16[256,1024]{1,0:T(8,128)(2,1)S(1)}, u32[]{:S(2)}, u32[]{:S(2)}) collective-permute-start(bf16[256,1024]{1,0:T(8,128)(2,1)S(1)} %get-tuple-element.32.rest_1_), channel_id=1, source_target_pairs={{0,24},{8,16},{16,8},{24,0},{1,25},{9,17},{17,9},{25,1},{2,26},{10... | collective-permute-start | bytes 1572872 | tf_op jit(solution)/shard_map/ppermute | solution.py:365
  94.8 8.7 %collective-permute-start.8 = (bf16[144,512]{1,0:T(8,128)(2,1)S(1)}, bf16[144,512]{1,0:T(8,128)(2,1)S(1)}, u32[]{:S(2)}, u32[]{:S(2)}) collective-permute-start(bf16[144,512]{1,0:T(8,128)(2,1)S(1)} %fusion), channel_id=1, source_target_pairs={{0,7},{1,2},{2,1},{3,4},{4,3},{5,6},{6,5},{7,0},{32,33},{33,32},{3... | collective-permute-start | bytes 442376 | tf_op jit(solution)/shard_map/ppermute | solution.py:374
  98.6 8.7 %collective-permute-start.11 = (bf16[144,512]{1,0:T(8,128)(2,1)S(1)}, bf16[144,512]{1,0:T(8,128)(2,1)S(1)}, u32[]{:S(2)}, u32[]{:S(2)}) collective-permute-start(bf16[144,512]{1,0:T(8,128)(2,1)S(1)} %fusion.1), channel_id=1, source_target_pairs={{0,7},{1,2},{2,1},{3,4},{4,3},{5,6},{6,5},{7,0},{32,33},{33,32},{3... | collective-permute-start | bytes 442376 | tf_op jit(solution)/shard_map/ppermute | solution.py:374
  104.0 6.9 %collective-permute-start.18 = (bf16[144,256]{1,0:T(8,128)(2,1)S(1)}, bf16[144,256]{1,0:T(8,128)(2,1)S(1)}, u32[]{:S(2)}, u32[]{:S(2)}) collective-permute-start(bf16[144,256]{1,0:T(8,128)(2,1)S(1)} %get-tuple-element.50.refs_0_), channel_id=1, source_target_pairs={{0,192},{64,128},{128,64},{192,0},{1,193},{65,129},{129,65},{193,1... | collective-permute-start | bytes 221192 | tf_op jit(solution)/shard_map/ppermute | solution.py:365
  106.6 7.1 %collective-permute-start.17 = (bf16[144,256]{1,0:T(8,128)(2,1)S(1)}, bf16[144,256]{1,0:T(8,128)(2,1)S(1)}, u32[]{:S(2)}, u32[]{:S(2)}) collective-permute-start(bf16[144,256]{1,0:T(8,128)(2,1)S(1)} %get-tuple-element.50.refs_0_), channel_id=1, source_target_pairs={{0,128},{64,192},{128,0},{192,64},{1,129},{65,193},{129,1},{193,65... | collective-permute-start | bytes 221192 | tf_op jit(solution)/shard_map/ppermute | solution.py:365
  107.1 6.6 %collective-permute-start.16 = (bf16[144,256]{1,0:T(8,128)(2,1)S(1)}, bf16[144,256]{1,0:T(8,128)(2,1)S(1)}, u32[]{:S(2)}, u32[]{:S(2)}) collective-permute-start(bf16[144,256]{1,0:T(8,128)(2,1)S(1)} %get-tuple-element.50.refs_0_), channel_id=1, source_target_pairs={{0,64},{64,0},{128,192},{192,128},{1,65},{65,1},{129,193},{193,129... | collective-permute-start | bytes 221192 | tf_op jit(solution)/shard_map/ppermute | solution.py:365
  107.8 9.8 %collective-permute-start.14 = (bf16[144,256]{1,0:T(8,128)(2,1)S(1)}, bf16[144,256]{1,0:T(8,128)(2,1)S(1)}, u32[]{:S(2)}, u32[]{:S(2)}) collective-permute-start(bf16[144,256]{1,0:T(8,128)(2,1)S(1)} %get-tuple-element.47.refs_0_), channel_id=1, source_target_pairs={{0,192},{64,128},{128,64},{192,0},{1,193},{65,129},{129,65},{193,1... | collective-permute-start | bytes 221192 | tf_op jit(solution)/shard_map/ppermute | solution.py:365
  110.4 7.3 %collective-permute-start.13 = (bf16[144,256]{1,0:T(8,128)(2,1)S(1)}, bf16[144,256]{1,0:T(8,128)(2,1)S(1)}, u32[]{:S(2)}, u32[]{:S(2)}) collective-permute-start(bf16[144,256]{1,0:T(8,128)(2,1)S(1)} %get-tuple-element.47.refs_0_), channel_id=1, source_target_pairs={{0,128},{64,192},{128,0},{192,64},{1,129},{65,193},{129,1},{193,65... | collective-permute-start | bytes 221192 | tf_op jit(solution)/shard_map/ppermute | solution.py:365
  110.9 6.7 %collective-permute-start.12 = (bf16[144,256]{1,0:T(8,128)(2,1)S(1)}, bf16[144,256]{1,0:T(8,128)(2,1)S(1)}, u32[]{:S(2)}, u32[]{:S(2)}) collective-permute-start(bf16[144,256]{1,0:T(8,128)(2,1)S(1)} %get-tuple-element.47.refs_0_), channel_id=1, source_target_pairs={{0,64},{64,0},{128,192},{192,128},{1,65},{65,1},{129,193},{193,129... | collective-permute-start | bytes 221192 | tf_op jit(solution)/shard_map/ppermute | solution.py:365
  113.7 6.0 %collective-permute-start.19 = (f32[144,256]{1,0:T(8,128)S(1)}, f32[144,256]{1,0:T(8,128)S(1)}, u32[]{:S(2)}, u32[]{:S(2)}) collective-permute-start(f32[144,256]{1,0:T(8,128)S(1)} %shard_map.108.mine_ref), channel_id=1, source_target_pairs={{0,32},{32,0},{1,33},{33,1},{2,34},{34,2},{3,35},{35,3},{4,36},{36... | collective-permute-start | bytes 442376 | tf_op jit(solution)/shard_map/ppermute | solution.py:365
  117.7 3.1 %collective-permute-start.15 = (f32[144,256]{1,0:T(8,128)S(1)}, f32[144,256]{1,0:T(8,128)S(1)}, u32[]{:S(2)}, u32[]{:S(2)}) collective-permute-start(f32[144,256]{1,0:T(8,128)S(1)} %shard_map.107.mine_ref), channel_id=1, source_target_pairs={{0,32},{32,0},{1,33},{33,1},{2,34},{34,2},{3,35},{35,3},{4,36},{36... | collective-permute-start | bytes 442376 | tf_op jit(solution)/shard_map/ppermute | solution.py:365
  (5 other events, 25.2 us)
Sparse Core Ops, SparseCore 0:
  9.8 42.4 all-gather.1
